TPU v7x, 256 devices: a whole 4x4x8 slice. The times are simulated.
256 devices in a mesh: mod: 4 (over x), tok: 16 (over z, core), tp: 4 (over y).
Axes of the slice: x: 4, y: 4, z: 8, core: 2. Of those that a mesh axis runs over, the one named last changes fastest.
Arguments:
- hidden_in: bfloat16 [2048, 8192], P('tok', 'tp'), may hold values from -19 to 19
- spans: int32 [128, 3], replicated, may hold values from 0 to 2048, as said below
- w_qkv: bfloat16 [4, 8192, 3, 64, 128], P('mod', 'tp', None, 'tok'), may hold values from -0.088388348 to 0.088388348
- w_out: bfloat16 [4, 64, 128, 8192], P('mod', 'tok', None, 'tp'), may hold values from -0.0625 to 0.0625
Outputs:
- section_out: bfloat16 [4, 1024, 8192], P('mod', 'tok', 'tp')
Inputs may be any that keep to these rules, and one draw needn't show every extreme that they name: `spans`: entries are the maximal runs of one modality, in order of start; starts and lengths are multiples of 16 and the runs cover the sequence. Unused entries have start 2048, length 0 and modality 0. Modality 0 holds exactly 1024 rows, every other modality at most that.
All inputs are finite; a program needn't handle non-finite values.
Results may differ from a plain program's by a relative error of at most 0.024.
Values may be sent and summed in bfloat16 or wider, within the bound.
A program may use at most 128 MiB of HBM per device.

v0:
```python
import jax
import jax.numpy as jnp
from jax import lax
from jax.sharding import PartitionSpec as P

big_negative = -1e30


def row_modalities(spans, seq_len):
    row_ids = jnp.arange(seq_len, dtype=jnp.int32)
    ends = spans[:, 0] + spans[:, 1]
    inside = (row_ids[:, None] >= spans[None, :, 0]) & (row_ids[:, None] < ends[None, :])
    return jnp.sum(jnp.where(inside, spans[None, :, 2], 0), axis=1)


def modality_slots(row_modality, capacity, modality):
    seq_len = row_modality.shape[0]
    row_ids = jnp.arange(seq_len, dtype=jnp.int32)
    chosen = row_modality == modality
    slot_index = jnp.cumsum(chosen.astype(jnp.int32)) - 1
    target = jnp.where(chosen, slot_index, capacity)
    source = jnp.zeros((capacity,), jnp.int32).at[target].set(row_ids, mode="drop")
    live_count = jnp.sum(chosen.astype(jnp.int32))
    is_valid = jnp.arange(capacity, dtype=jnp.int32) < live_count
    return (source, is_valid)


def attend_head(head_triple, query_pos, key_pos, score_scale):
    query_head, key_head, value_head = head_triple
    scores = (
        jnp.einsum("qe,ke->qk", query_head, key_head, preferred_element_type=jnp.float32)
        * score_scale
    )
    allowed = key_pos[None, :] <= query_pos[:, None]
    scores = jnp.where(allowed, scores, big_negative)
    running_top = jnp.max(scores, axis=1, keepdims=True)
    weights = jnp.exp(scores - running_top)
    weight_sum = jnp.sum(weights, axis=1, keepdims=True)
    mixture = jnp.dot(weights.astype(jnp.bfloat16), value_head, preferred_element_type=jnp.float32)
    return (mixture / weight_sum).astype(jnp.bfloat16)


def local(hidden_in, spans, w_qkv, w_out):
    sections = lax.axis_size("mod")
    tok_count = lax.axis_size("tok")
    section = lax.axis_index("mod")
    seq_len = hidden_in.shape[0] * tok_count
    capacity = seq_len // 2
    head_dim = w_qkv.shape[4]
    score_scale = head_dim ** (-0.5)
    local_qkv = w_qkv[0]
    row_modality = row_modalities(spans, seq_len)
    all_sources = []
    all_valid = []
    for modality in range(sections):
        source_m, valid_m = modality_slots(row_modality, capacity, modality)
        all_sources.append(source_m)
        all_valid.append(valid_m)
    source = jnp.stack(all_sources)[section]
    is_valid = jnp.stack(all_valid)[section]
    key_pos_all = jnp.concatenate(
        [jnp.where(all_valid[i], all_sources[i], seq_len) for i in range(sections)]
    )
    query_pos = jnp.where(is_valid, source, seq_len - 1)
    gathered = lax.all_gather(hidden_in, "tok", axis=0, tiled=True)
    picked = gathered[source]
    combined = lax.psum_scatter(
        jnp.einsum("rd,dkhe->hrke", picked, local_qkv, preferred_element_type=jnp.float32),
        "tp",
        scatter_dimension=0,
        tiled=True,
    ).astype(jnp.bfloat16)
    query_rows = combined[:, :, 0, :]
    key_rows = combined[:, :, 1, :]
    value_rows = combined[:, :, 2, :]
    all_keys, all_values = (
        lax.all_gather(key_rows, "mod", axis=1, tiled=True),
        lax.all_gather(value_rows, "mod", axis=1, tiled=True),
    )
    attended = lax.map(
        lambda triple: attend_head(triple, query_pos, key_pos_all, score_scale),
        (query_rows, all_keys, all_values),
    )
    heads_all = lax.all_gather(attended, "tp", axis=0, tiled=True)
    local_out = w_out[0]
    share_rows = capacity // tok_count
    first_row = lax.axis_index("tok") * share_rows
    projection = lax.psum_scatter(
        jnp.einsum("hre,hed->rd", heads_all, local_out, preferred_element_type=jnp.float32).astype(
            jnp.bfloat16
        ),
        "tok",
        scatter_dimension=0,
        tiled=True,
    ).astype(jnp.float32)
    my_source = lax.dynamic_slice_in_dim(source, first_row, share_rows)
    my_valid = lax.dynamic_slice_in_dim(is_valid, first_row, share_rows)
    residual = gathered[my_source].astype(jnp.float32)
    result = jnp.where(my_valid[:, None], residual + projection, 0.0).astype(jnp.bfloat16)
    return result[None]


def solution(mesh):
    in_specs = (P("tok", "tp"), P(), P("mod", "tp", None, "tok", None), P("mod", "tok", None, "tp"))
    out_specs = P("mod", "tok", "tp")
    return jax.shard_map(local, mesh=mesh, in_specs=in_specs, out_specs=out_specs, check_vma=False)
```

profile of v0, /device:TPU:1, one launch (start us, length us, event | category | flops | bytes accessed | tf_op | source)
XLA Modules:
  0.0 373.5 jit_solution(14918994338387387838)
XLA Ops:
  6.5 0.7 all-gather.8.cloned.1.call-update
  7.3 0.8 bitcast_add_fusion
  8.1 0.8 slice_bitcast_fusion.3
  9.2 0.7 convert_reduce_fusion.3
  11.5 1.3 dynamic-slice.2
  13.2 8.0 %scatter_custom_fusion.3 = s32[1024]{0:T(1024)S(1)} fusion(s32[2048]{0:T(1024)S(1)} %bitcast.101, s32[2048]{0:T(1024)S(1)} %iota.47, s32[]{:T(128)} %constant.75.clone.1), kind=kCustom, calls=%fused_computation.79 | custom fusion | bytes 4100 | tf_op jit(solution)/shard_map/scatter | solution.py:22
  21.3 8.0 %scatter_custom_fusion.2 = s32[1024]{0:T(1024)S(1)} fusion(s32[2048]{0:T(1024)S(1)} %bitcast.99, s32[2048]{0:T(1024)S(1)} %iota.46, s32[]{:T(128)} %constant.75.clone.1), kind=kCustom, calls=%fused_computation.81 | custom fusion | bytes 4100 | tf_op jit(solution)/shard_map/scatter | solution.py:22
  29.7 8.0 %scatter_custom_fusion.1 = s32[1024]{0:T(1024)S(1)} fusion(s32[2048]{0:T(1024)S(1)} %bitcast.102, s32[2048]{0:T(1024)S(1)} %iota.45, s32[]{:T(128)} %constant.75.clone.1), kind=kCustom, calls=%fused_computation.83 | custom fusion | bytes 4100 | tf_op jit(solution)/shard_map/scatter | solution.py:22
  37.8 8.0 %scatter_custom_fusion = s32[1024]{0:T(1024)S(1)} fusion(s32[2048]{0:T(1024)S(1)} %bitcast.100, s32[2048]{0:T(1024)S(1)} %iota.44, s32[]{:T(128)} %constant.75.clone.1), kind=kCustom, calls=%fused_computation.85 | custom fusion | bytes 4100 | tf_op jit(solution)/shard_map/scatter | solution.py:22
  45.9 23.5 %all-gather.8.cloned.1.call-done = bf16[2048,2048]{1,0:T(8,128)(2,1)} async-done(((bf16[128,2048]{1,0:T(8,128)(2,1)}), bf16[2048,2048]{1,0:T(8,128)(2,1)}) %all-gather.8.cloned.1.call-update) | async-done | bytes 8388624 | tf_op jit(solution)/shard_map/all_gather | solution.py:65
  69.4 13.3 %gather_fusion.1 = bf16[1024,2048]{1,0:T(8,128)(2,1)} fusion(bf16[2048,2048]{1,0:T(8,128)(2,1)} %all-gather.8.cloned.1.call-done, s32[1024]{0:T(1024)S(1)} %broadcast_clamp_fusion), kind=kCustom, calls=%fused_computation.1 | custom fusion | bytes 8392704 | tf_op jit(solution)/shard_map/gather | solution.py:66
  82.7 12.0 %fusion.8 = f32[4,1024,3,128]{3,1,0,2:T(8,128)} fusion(bf16[2048,3,4,128]{3,2,1,0:T(4,128)(2,1)} %bitcast.103, bf16[1024,2048]{1,0:T(8,128)(2,1)} %gather_fusion.1), kind=kOutput, calls=%fused_computation.16 | convolution fusion | flops 6442450944 | bytes 16777216 | tf_op jit(solution)/shard_map/rd,dkhe->hrke/dot_general | solution.py:68
  94.6 113.4 %all-reduce.2 = bf16[4,1024,3,128]{3,1,0,2:T(8,128)(2,1)} all-reduce(f32[4,1024,3,128]{3,1,0,2:T(8,128)} %fusion.8), channel_id=5, replica_groups=mesh['mod'=4,'tok'=16,'tp'=4] {'tp'}, use_global_device_ids=true, to_apply=%region_17.18.clone | all-reduce | flops 1572864 | bytes 9437184
  208.0 1.8 dynamic-slice_convert_fusion
  209.8 0.8 fusion.44
  210.8 1.2 iota_compare_fusion.6
  212.0 1.2 iota_compare_fusion.8
  213.2 0.6 fusion.32
  213.8 0.6 fusion.31
  214.4 0.6 fusion.30
  215.0 0.6 fusion.29
  215.9 18.5 %all-gather.10.cloned.1.call-done = bf16[1,4096,1,128]{3,1,0,2:T(8,128)(2,1)} async-done(((bf16[1,1024,1,128]{3,1,0,2:T(8,128)(2,1)}), bf16[1,4096,1,128]{3,1,0,2:T(8,128)(2,1)}) %all-gather.10.cloned.1.call-update) | async-done | bytes 1048592 | tf_op jit(solution)/shard_map/all_gather | solution.py:77
  234.5 4.2 %fusion.2 = (f32[1024]{0:T(1024)S(1)}, f32[1024,4096]{1,0:T(8,128)S(1)}) fusion(s32[4096]{0:T(1024)S(1)} %pad_add_fusion.1, s32[1024]{0:T(1024)S(1)} %bitcast.95, bf16[1,4096,1,128]{3,1,0,2:T(8,128)(2,1)} %all-gather.10.cloned.1.call-done, bf16[1,1024,3,128]{3,1,0,2:T(8,128)(2,1)S(1)} %dynamic-slice_convert_fusion), kind=kOutput, calls=%fused_computation.10 | convolution fusion | flops 1090518016 | bytes 18112512 | tf_op jit(solution)/shard_map/while/body/eval_jaxpr/qe,ke->qk/dot_general | solution.py:31
  238.7 5.7 %copy-done.1 = f32[1024,4096]{1,0:T(8,128)} copy-done((f32[1024,4096]{1,0:T(8,128)}, f32[1024,4096]{1,0:T(8,128)S(1)}, u32[]{:S(2)}) %copy-start.1) | copy-done | bytes 16777240
  244.4 4.7 %fusion = f32[1024]{0:T(1024)S(1)} fusion(f32[1024,4096]{1,0:T(8,128)S(1)} %get-tuple-element.45, f32[1024]{0:T(1024)S(1)} %get-tuple-element.44, s32[4096]{0:T(1024)S(1)} %pad_add_fusion.1, s32[1024]{0:T(1024)S(1)} %bitcast.96), kind=kLoop, calls=%fused_computation.8 | loop fusion | flops 20970496 | bytes 16805888 | tf_op jit(solution)/shard_map/while/body/eval_jaxpr/reduce_sum | solution.py:38
  249.2 14.0 %all-gather.12.cloned.1.call-done = bf16[1,4096,1,128]{3,1,0,2:T(8,128)(2,1)} async-done(((bf16[1,1024,1,128]{3,1,0,2:T(8,128)(2,1)}), bf16[1,4096,1,128]{3,1,0,2:T(8,128)(2,1)}) %all-gather.12.cloned.1.call-update) | async-done | bytes 1048592 | tf_op jit(solution)/shard_map/all_gather | solution.py:78
  263.2 8.8 %fusion.23 = bf16[1024,128]{1,0:T(8,128)(2,1)} fusion(bf16[1,4096,1,128]{3,1,0,2:T(8,128)(2,1)} %all-gather.12.cloned.1.call-done, f32[1024,4096]{1,0:T(8,128)} %copy-done.1, f32[1024]{0:T(1024)S(1)} %get-tuple-element.44, s32[4096]{0:T(1024)S(1)} %pad_add_fusion.1, s32[1024]{0:T(1024)S(1)} %bitcast.97, f32[1024]{0:T(1024)S(1)} %fusion), kind=kOutput, calls=%fused_computation.27 | convolution fusion | flops 1094975488 | bytes 18116608 | tf_op jit(solution)/shard_map/while/body/eval_jaxpr/dot_general | solution.py:39
  272.0 27.0 %all-gather.14.cloned.1.call-done = bf16[4096,128]{1,0:T(8,128)(2,1)} async-done(((bf16[1024,128]{1,0:T(8,128)(2,1)}), bf16[4096,128]{1,0:T(8,128)(2,1)}) %all-gather.14.cloned.1.call-update) | async-done | bytes 1048592 | tf_op jit(solution)/shard_map/all_gather | solution.py:84
  299.0 5.1 %bitcast_convert_fusion = bf16[1024,2048]{1,0:T(8,128)(2,1)} fusion(bf16[4,1024,128]{2,1,0:T(8,128)(2,1)} %bitcast.104, bf16[1,4,128,2048]{3,2,1,0:T(8,128)(2,1)S(1)} %copy-done), kind=kOutput, calls=%fused_computation.11 | convolution fusion | flops 2149580800 | bytes 7340032 | tf_op jit(solution)/shard_map/hre,hed->rd/dot_general | solution.py:89
  304.3 5.4 %gather_fusion = bf16[64,2048]{1,0:T(8,128)(2,1)S(1)} fusion(bf16[2048,2048]{1,0:T(8,128)(2,1)} %all-gather.8.cloned.1.call-done, s32[1024]{0:T(1024)S(1)} %pad_clamp_fusion), kind=kCustom, calls=%fused_computation | custom fusion | bytes 524544 | tf_op jit(solution)/shard_map/gather | solution.py:98
  309.8 55.4 %reduce-scatter.5.cloned.1.call-done = bf16[64,2048]{1,0:T(8,128)(2,1)} async-done(((bf16[1024,2048]{1,0:T(8,128)(2,1)}), bf16[64,2048]{1,0:T(8,128)(2,1)}) %reduce-scatter.5.cloned.1.call-update) | async-done | bytes 262160 | tf_op jit(solution)/shard_map/reduce_scatter | solution.py:88
  365.2 1.7 fusion.28
  (52 shorter events, 3.4 us)
Async XLA Ops:
  6.5 292.5 %copy-start = (bf16[1,4,128,2048]{3,2,1,0:T(8,128)(2,1)S(1)}, bf16[1,4,128,2048]{3,2,1,0:T(8,128)(2,1)}, u32[]{:S(2)}) copy-start(bf16[1,4,128,2048]{3,2,1,0:T(8,128)(2,1)} %param.7) | copy-start | bytes 6291460
  6.5 62.9 %all-gather.8.cloned.1.call-start = ((), (), s32[]{:S(2)}) async-start(), calls=%async_computation.1 | async-start | bytes 8912896 | tf_op jit(solution)/shard_map/all_gather | solution.py:65
  7.3 227.2 %all-gather.10.cloned.1.call-start = ((), (), s32[]{:S(2)}) async-start(), calls=%async_computation.3 | async-start | bytes 1310720 | tf_op jit(solution)/shard_map/all_gather | solution.py:77
  210.7 52.5 %all-gather.12.cloned.1.call-start = ((), (), s32[]{:S(2)}) async-start(), calls=%async_computation.4 | async-start | bytes 1310720 | tf_op jit(solution)/shard_map/all_gather | solution.py:78
  215.7 83.3 %all-gather.14.cloned.1.call-start = ((), (), s32[]{:S(2)}) async-start(), calls=%async_computation.5 | async-start | bytes 1310720 | tf_op jit(solution)/shard_map/all_gather | solution.py:84
  238.7 5.7 %copy-start.1 = (f32[1024,4096]{1,0:T(8,128)}, f32[1024,4096]{1,0:T(8,128)S(1)}, u32[]{:S(2)}) copy-start(f32[1024,4096]{1,0:T(8,128)S(1)} %get-tuple-element.45) | copy-start | bytes 50331652
  272.0 93.2 %reduce-scatter.5.cloned.1.call-start = ((), (), s32[]{:S(2)}) async-start(), calls=%async_computation.2 | async-start | bytes 4456448 | tf_op jit(solution)/shard_map/reduce_scatter | solution.py:88
Sparse Core Ops, SparseCore 0:
  9.2 60.1 all-gather.7
  210.8 23.6 all-gather.9
  236.3 26.8 all-gather.11
  272.1 26.8 all-gather.13
  304.3 60.8 reduce-scatter.4
where the time goes:
time: 376 us; the launch traced here: 373 us
  waiting for transfers between devices  139 us (37%)
  blocking collectives  113 us (30%)
  local copies, waits for them, and re-layouts  62.1 us (17%)
  matrix products  30 us (8%)
  other arithmetic  14.9 us (4%)
  between operations  13.4 us (4%)
    unnamed x1, blocking collectives  113 us
    reduce_scatter x1, waiting for transfers between devices, local(): lax.psum_scatter(jnp.einsum('hre,hed->rd', heads_all, local_out, preferre...  55.4 us
    scatter x4, local copies, waits for them, and re-layouts, modality_slots(): jnp.zeros((capacity,), jnp.int32).at[target].set(row_ids, mode='drop')  32.2 us
    all_gather x1, waiting for transfers between devices, local(): heads_all = lax.all_gather(attended, 'tp', axis=0, tiled=True)  27 us
    all_gather x1, waiting for transfers between devices, local(): gathered = lax.all_gather(hidden_in, 'tok', axis=0, tiled=True)  23.5 us
    all_gather x1, waiting for transfers between devices, local(): lax.all_gather(key_rows, 'mod', axis=1, tiled=True)  18.5 us
    all_gather x1, waiting for transfers between devices, local(): lax.all_gather(value_rows, 'mod', axis=1, tiled=True)  14 us
    gather x1, local copies, waits for them, and re-layouts, local(): picked = gathered[source]  13.3 us
  transfers between devices with their start and end apart: 5, of which 5 were waited for; matrix products, arithmetic and copies ran while one was open for 16% of the time, Pallas kernels for 0%

commit v1 on v0

v1 whole, which is shorter than its diff:
```python
import jax
import jax.numpy as jnp
from jax import lax
from jax.experimental import pallas as pl
from jax.experimental.pallas import tpu as pltpu
from jax.sharding import PartitionSpec as P

MESH = pl.DeviceIdType.MESH
UNIT = 16
NEG = -1e30


def remote(src, dst, send, recv, dev):
    return pltpu.make_async_remote_copy(
        src_ref=src, dst_ref=dst, send_sem=send, recv_sem=recv, device_id=dev, device_id_type=MESH
    )


def greet(devs):
    barrier = pltpu.get_barrier_semaphore()
    for dev in devs:
        pl.semaphore_signal(barrier, inc=1, device_id=dev, device_id_type=MESH)
    pl.semaphore_wait(barrier, len(devs))


def where_am_i():
    t = lax.axis_index("tok")
    return lax.axis_index("mod"), lax.div(t, 2), lax.rem(t, 2), lax.axis_index("tp")


def project_kernel(
    src_ref, hid_ref, w_ref,
    q_ref, kv_ref, res_ref,
    xg, wv, y, yc, sbuf, rbuf,
    local_sem, z_send, z_recv, x_send, x_recv, c_send, c_recv, own_sem,
    rs_send, rs_recv, g_send, g_recv, f_send, f_recv,
):
    xm, z, c, yp = where_am_i()
    half = lax.rem(xm, 2)
    zdev = [{"tok": lax.rem(z + 1, 8) * 2 + c}, {"tok": lax.rem(z + 7, 8) * 2 + c}]
    xdev = [{"mod": lax.rem(xm + 1, 4)}, {"mod": lax.rem(xm + 3, 4)}]
    ydev = [{"tp": lax.rem(yp + 1, 4)}, {"tp": lax.rem(yp + 3, 4)}]
    cdev = {"tok": z * 2 + 1 - c}

    def region(zz, cc, hh, s):
        units = pl.ds((zz * 2 + cc) * 8, 8)
        return xg.at[units, :, pl.ds(pl.multiple_of(hh * 1024 + s * 512, 512), 512)]

    def own_rows(cc):
        return xg.at[pl.ds((z * 2 + cc) * 8, 8)]

    def block_at(way, d):
        return lax.rem(z + 8 - d, 8) if way == 0 else lax.rem(z + d, 8)

    hid_copy = pltpu.make_async_copy(hid_ref, own_rows(c), local_sem.at[0])
    hid_copy.start()
    w_copy = pltpu.make_async_copy(w_ref, wv, local_sem.at[1])
    w_copy.start()
    greet(zdev + xdev + ydev + [cdev])
    hid_copy.wait()

    sent = []

    def send(src, dst, ssem, rsem, dev):
        copy = remote(src, dst, ssem, rsem, dev)
        copy.start()
        sent.append(copy)

    for s in range(2):
        for way in range(2):
            reg = region(z, c, half, s)
            send(reg, reg, z_send.at[way, 0, s], z_recv.at[way, 0, s], zdev[way])
    send(own_rows(c), own_rows(c), own_sem.at[0], own_sem.at[1], cdev)

    def multiply(zz):
        units = pl.ds(zz * 16, 16)

        def step(j, carry):
            cols = pl.ds(pl.multiple_of(j * 256, 256), 256)
            value = jnp.dot(
                xg[units].reshape(256, 2048), wv[:, cols], preferred_element_type=jnp.float32
            )
            y[units, :, cols] = value.astype(jnp.bfloat16).reshape(16, UNIT, 256)
            return carry

        lax.fori_loop(0, 6, step, 0)

    w_copy.wait()
    remote(own_rows(1 - c), own_rows(1 - c), own_sem.at[0], own_sem.at[1], cdev).wait_recv()
    multiply(z)

    events = []
    for d in range(1, 5):
        for s in range(2):
            for way in range(2):
                if d < 4 or s == way:
                    events.append((way, d, s))

    def from_x(ev):
        way, d, s = ev
        reg = region(block_at(way, d), c, 1 - half, s)
        remote(reg, reg, x_send.at[way, d - 1, s], x_recv.at[way, d - 1, s], xdev[s]).wait_recv()
        send(reg, reg, c_send.at[way, d - 1, s, 1], c_recv.at[way, d - 1, s, 1], cdev)

    def from_core(way, d):
        for s in range(2):
            w = s if d == 4 else way
            for o in range(2):
                hh = half if o == 0 else 1 - half
                reg = region(block_at(way, d), 1 - c, hh, s)
                remote(reg, reg, c_send.at[w, d - 1, s, o], c_recv.at[w, d - 1, s, o], cdev).wait_recv()

    for k, ev in enumerate(events):
        way, d, s = ev
        reg = region(block_at(way, d), c, half, s)
        remote(reg, reg, z_send.at[way, d - 1, s], z_recv.at[way, d - 1, s], zdev[way]).wait_recv()
        if d < 3 or (d == 3 and s == way):
            send(reg, reg, z_send.at[way, d, s], z_recv.at[way, d, s], zdev[way])
        send(reg, reg, x_send.at[way, d - 1, s], x_recv.at[way, d - 1, s], xdev[s])
        send(reg, reg, c_send.at[way, d - 1, s, 0], c_recv.at[way, d - 1, s, 0], cdev)
        if k >= 2:
            from_x(events[k - 2])
        if k in (5, 9):
            from_core(0, k // 4)
            multiply(block_at(0, k // 4))
        if k in (7, 11):
            from_core(1, k // 4)
            multiply(block_at(1, k // 4))
    from_x(events[-2])
    from_x(events[-1])
    for way in range(2):
        from_core(way, 3)
        multiply(block_at(way, 3))
    from_core(0, 4)
    multiply(block_at(0, 4))

    t = z * 2 + c
    for i in range(4):
        res_ref[i * UNIT:(i + 1) * UNIT, :] = xg[src_ref[t * 4 + i]]

    def compact(i, carry):
        to = pl.ds(pl.multiple_of(i * UNIT, UNIT), UNIT)
        rows = y[src_ref[i]]
        for j in range(12):
            yc[j, to, :] = rows[:, j * 128:(j + 1) * 128]
        return carry

    lax.fori_loop(0, 64, compact, 0)

    kinds = (1, 2, 0)
    turn = (1, 3)

    def rows_of(way, sub):
        return pl.ds(way * 512 + sub * 256, 256)

    def add(kind, dest, way, sub, step):
        return (
            yc[kind * 4 + dest, rows_of(way, sub), :].astype(jnp.float32)
            + rbuf[way, kind, sub, step].astype(jnp.float32)
        ).astype(jnp.bfloat16)

    def arrived(kind, way, sub, step):
        remote(
            rbuf.at[way, kind, sub, step], rbuf.at[way, kind, sub, step],
            rs_send.at[way, kind, sub, step], rs_recv.at[way, kind, sub, step], ydev[way],
        ).wait_recv()

    def hop(kind, step):
        for sub in range(2):
            for way in range(2):
                dest = lax.rem(yp + 4 * 3 - turn[way] * (step + 1), 4)
                if step == 0:
                    src = yc.at[kind * 4 + dest, rows_of(way, sub), :]
                else:
                    arrived(kind, way, sub, step - 1)
                    sbuf[way, kind, sub, step - 1] = add(kind, dest, way, sub, step - 1)
                    src = sbuf.at[way, kind, sub, step - 1]
                send(
                    src, rbuf.at[way, kind, sub, step],
                    rs_send.at[way, kind, sub, step], rs_recv.at[way, kind, sub, step], ydev[way],
                )

    def kv_rows(section, kind, way, sub):
        return kv_ref.at[kind - 1, pl.ds(section * 64 + way * 32 + sub * 16, 16)]

    def final(kind):
        for sub in range(2):
            for way in range(2):
                arrived(kind, way, sub, 2)
                value = add(kind, yp, way, sub, 2)
                if kind == 0:
                    q_ref[rows_of(way, sub), :] = value
                else:
                    reg = kv_rows(xm, kind, way, sub)
                    reg[...] = value.reshape(16, UNIT, 128)
                    for o in range(2):
                        send(
                            reg, reg, g_send.at[o, kind - 1, way, sub],
                            g_recv.at[o, kind - 1, way, sub], xdev[o],
                        )

    def spread(kind):
        for sub in range(2):
            for way in range(2):
                reg = kv_rows(lax.rem(xm + (3, 1)[way], 4), kind, way, sub)
                remote(
                    reg, reg, g_send.at[way, kind - 1, way, sub],
                    g_recv.at[way, kind - 1, way, sub], xdev[way],
                ).wait_recv()
                send(
                    reg, reg, f_send.at[kind - 1, way, sub],
                    f_recv.at[kind - 1, way, sub], xdev[way],
                )

    hop(1, 0)
    hop(1, 1)
    hop(1, 2)
    hop(2, 0)
    final(1)
    hop(2, 1)
    hop(2, 2)
    hop(0, 0)
    final(2)
    spread(1)
    hop(0, 1)
    hop(0, 2)
    spread(2)
    final(0)
    for kind in (1, 2):
        for sub in range(2):
            for way in range(2):
                reg = kv_rows(lax.rem(xm + (1, 3)[way], 4), kind, way, sub)
                remote(
                    reg, reg, g_send.at[1 - way, kind - 1, way, sub],
                    g_recv.at[1 - way, kind - 1, way, sub], xdev[1 - way],
                ).wait_recv()
                reg = kv_rows(lax.rem(xm + 2, 4), kind, way, sub)
                remote(
                    reg, reg, f_send.at[kind - 1, way, sub],
                    f_recv.at[kind - 1, way, sub], xdev[way],
                ).wait_recv()
    for copy in sent:
        copy.wait_send()


def attend_kernel(
    src_ref, slot_ref, live_ref, q_ref, kv_ref, wo_ref, res_ref,
    out_ref,
    kt, vt, heads, zown, csend, crecv, rsend, rrecv,
    h_send, h_recv, c_send_sem, c_recv_sem, r_send_sem, r_recv_sem,
):
    xm, z, c, yp = where_am_i()
    zdev = [{"tok": lax.rem(z + 1, 8) * 2 + c}, {"tok": lax.rem(z + 7, 8) * 2 + c}]
    ydev = [{"tp": lax.rem(yp + k, 4)} for k in (1, 2, 3)]
    cdev = {"tok": z * 2 + 1 - c}
    greet(zdev + ydev + [cdev])

    def order_keys(u, carry):
        to = pl.ds(pl.multiple_of(u * UNIT, UNIT), UNIT)
        unit = slot_ref[u]
        kt[to, :] = kv_ref[0, unit]
        vt[to, :] = kv_ref[1, unit]
        return carry

    lax.fori_loop(0, 128, order_keys, 0)

    dests = [lax.rem(z + k, 8) for k in (4, 3, 5, 2, 6, 1, 7, 0)]
    sent = []

    def send(src, dst, ssem, rsem, dev):
        copy = remote(src, dst, ssem, rsem, dev)
        copy.start()
        sent.append(copy)

    def my_cols(p):
        return pl.ds(pl.multiple_of(p * 128, 128), 128)

    def attend(i):
        d = dests[i]
        query = q_ref[pl.ds(pl.multiple_of(d * 128, 128), 128), :]
        scores = lax.dot_general(
            query, kt[...], (((1,), (1,)), ((), ())), preferred_element_type=jnp.float32
        ) * (128 ** -0.5)
        base = jnp.concatenate(
            [jnp.full((UNIT, 1), src_ref[d * 8 + k] * UNIT, jnp.int32) for k in range(8)], axis=0
        )
        row = lax.broadcasted_iota(jnp.int32, (128, 1), 0)
        pos = base + lax.rem(row, UNIT)
        key = lax.broadcasted_iota(jnp.int32, (128, 2048), 1)
        scores = jnp.where(key <= pos, scores, NEG)
        top = jnp.max(scores, axis=1, keepdims=True)
        weights = jnp.exp(scores - top)
        total = jnp.sum(weights, axis=1, keepdims=True)
        mixed = jnp.dot(weights.astype(jnp.bfloat16), vt[...], preferred_element_type=jnp.float32)
        heads[i, :, my_cols(yp)] = (mixed / total).astype(jnp.bfloat16)
        mine = heads.at[i, :, my_cols(yp)]
        for k in range(3):
            send(mine, mine, h_send.at[i, k], h_recv.at[i, k], ydev[k])

    def project(i):
        for k in range(3):
            other = heads.at[i, :, my_cols(lax.rem(yp + 3 - k, 4))]
            remote(other, other, h_send.at[i, k], h_recv.at[i, k], ydev[k]).wait_recv()
        def part(j, carry):
            cols = pl.ds(pl.multiple_of(j * 512, 512), 512)
            value = jnp.dot(heads[i], wo_ref[:, cols], preferred_element_type=jnp.float32)
            first = value[:64]
            second = value[64:]
            zown[i, :, cols] = jnp.where(c == 0, first, second)
            csend[i, :, cols] = jnp.where(c == 0, second, first).astype(jnp.bfloat16)
            return carry

        lax.fori_loop(0, 4, part, 0)
        send(csend.at[i], crecv.at[i], c_send_sem.at[i], c_recv_sem.at[i], cdev)

    top_of = {(0, 0): 3, (0, 1): 4, (1, 0): 4, (1, 1): 3}

    def ring(way, dist, part):
        i = {4: 0, 3: 1, 2: 3, 1: 5}[dist] + (1 if way == 1 and dist < 4 else 0)
        cols = slice(part * 1024, part * 1024 + 1024)
        value = zown[i, :, cols] + crecv[i, :, cols].astype(jnp.float32)
        if dist < top_of[(way, part)]:
            came = rrecv.at[way, dist, part]
            remote(
                came, came, r_send_sem.at[way, dist, part], r_recv_sem.at[way, dist, part], zdev[way]
            ).wait_recv()
            value = value + came[...].astype(jnp.float32)
        rsend[way, dist - 1, part] = value.astype(jnp.bfloat16)
        send(
            rsend.at[way, dist - 1, part], rrecv.at[way, dist - 1, part],
            r_send_sem.at[way, dist - 1, part], r_recv_sem.at[way, dist - 1, part], zdev[way],
        )

    def core_sum(i):
        remote(crecv.at[i], crecv.at[i], c_send_sem.at[i], c_recv_sem.at[i], cdev).wait_recv()

    def pass_on(i):
        core_sum(i)
        if i == 0:
            ring(1, 4, 0)
            ring(0, 4, 1)
        elif i < 7:
            way = (i - 1) % 2
            dist = 3 - (i - 1) // 2
            for part in ((0, 1) if way == 0 else (1, 0)):
                ring(way, dist, part)

    for i in range(8):
        attend(i)
        if i >= 1:
            project(i - 1)
        if i >= 2:
            pass_on(i - 2)
    project(7)
    pass_on(6)
    core_sum(7)

    t = z * 2 + c
    live_rows = live_ref[0] * UNIT
    for part in range(2):
        cols = slice(part * 1024, part * 1024 + 1024)
        value = zown[7, :, cols] + crecv[7, :, cols].astype(jnp.float32)
        for way in range(2):
            came = rrecv.at[way, 0, part]
            remote(
                came, came, r_send_sem.at[way, 0, part], r_recv_sem.at[way, 0, part], zdev[way]
            ).wait_recv()
            value = value + came[...].astype(jnp.float32)
        value = value + res_ref[:, cols].astype(jnp.float32)
        row = lax.broadcasted_iota(jnp.int32, (64, 1024), 0) + t * 64
        out_ref[:, cols] = jnp.where(row < live_rows, value, 0.0).astype(jnp.bfloat16)
    for copy in sent:
        copy.wait_send()


def plan(spans):
    units = spans.shape[0]
    ids = jnp.arange(units, dtype=jnp.int32)
    at = ids * UNIT
    ends = spans[:, 0] + spans[:, 1]
    inside = (at[:, None] >= spans[None, :, 0]) & (at[:, None] < ends[None, :])
    unit_mod = jnp.sum(jnp.where(inside, spans[None, :, 2], 0), axis=1)
    before = (unit_mod[:, None] == unit_mod[None, :]) & (ids[None, :] < ids[:, None])
    rank = jnp.sum(before.astype(jnp.int32), axis=1)
    slot = unit_mod * 64 + rank
    mine = unit_mod == lax.axis_index("mod")
    here = mine[None, :] & (rank[None, :] == jnp.arange(64, dtype=jnp.int32)[:, None])
    src = jnp.sum(jnp.where(here, ids[None, :], 0), axis=1)
    live = jnp.sum(mine.astype(jnp.int32)).reshape(1)
    return src, slot, live


def local(hidden_in, spans, w_qkv, w_out):
    src, slot, live = plan(spans)
    w = w_qkv[0].reshape(2048, 1536)
    wo = w_out.reshape(512, 2048)
    bf = jnp.bfloat16
    dma = pltpu.SemaphoreType.DMA
    vmem = pl.BlockSpec(memory_space=pltpu.VMEM)
    smem = pl.BlockSpec(memory_space=pltpu.SMEM)
    anyw = pl.BlockSpec(memory_space=pl.ANY)
    q, kv, res = pl.pallas_call(
        project_kernel,
        out_shape=(
            jax.ShapeDtypeStruct((1024, 128), bf),
            jax.ShapeDtypeStruct((2, 256, UNIT, 128), bf),
            jax.ShapeDtypeStruct((64, 2048), bf),
        ),
        in_specs=[smem, anyw, anyw],
        out_specs=(vmem, vmem, vmem),
        scratch_shapes=[
            pltpu.VMEM((128, UNIT, 2048), bf),
            pltpu.VMEM((2048, 1536), bf),
            pltpu.VMEM((128, UNIT, 1536), bf),
            pltpu.VMEM((12, 1024, 128), bf),
            pltpu.VMEM((2, 3, 2, 2, 256, 128), bf),
            pltpu.VMEM((2, 3, 2, 3, 256, 128), bf),
            dma((2,)),
            dma((2, 4, 2)), dma((2, 4, 2)),
            dma((2, 4, 2)), dma((2, 4, 2)),
            dma((2, 4, 2, 2)), dma((2, 4, 2, 2)),
            dma((2,)),
            dma((2, 3, 2, 3)), dma((2, 3, 2, 3)),
            dma((2, 2, 2, 2)), dma((2, 2, 2, 2)),
            dma((2, 2, 2)), dma((2, 2, 2)),
        ],
        compiler_params=pltpu.CompilerParams(
            collective_id=1, has_side_effects=True, vmem_limit_bytes=56 * 1024 * 1024
        ),
        name="project",
    )(src, hidden_in.reshape(8, UNIT, 2048), w)
    out = pl.pallas_call(
        attend_kernel,
        out_shape=jax.ShapeDtypeStruct((64, 2048), bf),
        in_specs=[smem, smem, smem, vmem, vmem, vmem, vmem],
        out_specs=vmem,
        scratch_shapes=[
            pltpu.VMEM((2048, 128), bf),
            pltpu.VMEM((2048, 128), bf),
            pltpu.VMEM((8, 128, 512), bf),
            pltpu.VMEM((8, 64, 2048), jnp.float32),
            pltpu.VMEM((8, 64, 2048), bf),
            pltpu.VMEM((8, 64, 2048), bf),
            pltpu.VMEM((2, 4, 2, 64, 1024), bf),
            pltpu.VMEM((2, 4, 2, 64, 1024), bf),
            dma((8, 3)), dma((8, 3)),
            dma((8,)), dma((8,)),
            dma((2, 4, 2)), dma((2, 4, 2)),
        ],
        compiler_params=pltpu.CompilerParams(
            collective_id=2, has_side_effects=True, vmem_limit_bytes=56 * 1024 * 1024
        ),
        name="attend",
    )(src, slot, live, q, kv, wo, res)
    return out[None]


def solution(mesh):
    in_specs = (P("tok", "tp"), P(), P("mod", "tp", None, "tok", None), P("mod", "tok", None, "tp"))
    out_specs = P("mod", "tok", "tp")
    return jax.shard_map(local, mesh=mesh, in_specs=in_specs, out_specs=out_specs, check_vma=False)
```

time: 376 us -> 153 us (0.41)
  waiting for transfers between devices: 139 us -> 0 us
  Pallas kernels: 0 us -> 136 us
  blocking collectives: 113 us -> 0 us
  local copies, waits for them, and re-layouts: 62.1 us -> 13.4 us
  matrix products: 30 us -> 0 us
  between operations: 13.4 us -> 0.03 us
  other arithmetic: 14.9 us -> 2.97 us
    pallas_call x0 -> x2, Pallas kernels: none -> 136 us  [the longest x1 90.7 us: local(): pl.pallas_call(project_kernel, out_shape=(jax.ShapeDtypeStruct((1024, 128...]
    unnamed x1 -> x0, blocking collectives: 113 us -> none
    all_gather x4 -> x0, waiting for transfers between devices: 83.1 us -> none  [the longest x1 27 us: local(): heads_all = lax.all_gather(attended, 'tp', axis=0, tiled=True)]
    reduce_scatter x1 -> x0, waiting for transfers between devices: 55.4 us -> none  [local(): lax.psum_scatter(jnp.einsum('hre,hed->rd', heads_all, local_out, preferre...]
    scatter x4 -> x0, local copies, waits for them, and re-layouts: 32.2 us -> none  [modality_slots(): jnp.zeros((capacity,), jnp.int32).at[target].set(row_ids, mode='drop')]
    dot_general x4 -> x0, matrix products: 30 us -> none  [the longest x1 12 us: local(): jnp.einsum('rd,dkhe->hrke', picked, local_qkv, preferred_element_type=jnp...]
    gather x2 -> x0, local copies, waits for them, and re-layouts: 18.7 us -> none  [the longest x1 13.3 us: local(): picked = gathered[source]]
    another operation x7 -> x1, local copies, waits for them, and re-layouts: 0.68 us -> 11 us  [local(): w = w_qkv[0].reshape(2048, 1536)]
  transfers between devices with their start and end apart: 5 -> 0, of which waited for: 5 -> 0; matrix products, arithmetic and copies ran while one was open for 16% -> 0% of each run, Pallas kernels for 0% -> 0%
where the time goes in v1:
time: 153 us
  Pallas kernels  136 us (89%)
  local copies, waits for them, and re-layouts  13.4 us (9%)
  other arithmetic  2.97 us (2%)
    pallas_call x1, Pallas kernels, local(): pl.pallas_call(project_kernel, out_shape=(jax.ShapeDtypeStruct((1024, 128...  90.7 us
    pallas_call x1, Pallas kernels, local(): pl.pallas_call(attend_kernel, out_shape=jax.ShapeDtypeStruct((64, 2048),...  45.4 us
    another operation x1, local copies, waits for them, and re-layouts, local(): w = w_qkv[0].reshape(2048, 1536)  11 us

profile of v1, /device:TPU:1, one launch (start us, length us, event | category | flops | bytes accessed | tf_op | source)
XLA Modules:
  0.0 152.6 jit_solution(1505486443971438220)
XLA Ops:
  0.0 0.8 slice_bitcast_fusion.1
  0.8 0.8 bitcast_add_fusion
  1.5 0.2 select_reduce_fusion
  1.7 0.2 convert_reduce_fusion
  1.9 1.2 convert_reduce_fusion.1
  3.1 0.7 select_reduce_fusion.1.src_ref
  3.7 11.0 %reshape_squeeze.3.w_ref = bf16[2048,1536]{1,0:T(8,128)(2,1)} reshape(bf16[1,2048,3,4,128]{4,3,2,1,0:T(4,128)(2,1)} %param.6) | data formatting | bytes 12582912 | tf_op jit(solution)/shard_map/reshape;squeeze | solution.py:395
  14.7 90.7 %project.1 = (bf16[1024,128]{1,0:T(8,128)(2,1)}, bf16[2,256,16,128]{3,2,1,0:T(8,128)(2,1)}, bf16[64,2048]{1,0:T(8,128)(2,1)}) custom-call(s32[64]{0:T(128)} %select_reduce_fusion.1.src_ref, bf16[8,16,2048]{2,1,0:T(8,128)(2,1)} %bitcast.14, bf16[2048,1536]{1,0:T(8,128)(2,1)} %reshape_squeeze.3.w_ref), custom_call_target="tpu_custom_call" | custom-call | tf_op jit(solution)/shard_map/project/pallas_call | solution.py:402
  105.5 45.4 %attend.1 = bf16[64,2048]{1,0:T(8,128)(2,1)} custom-call(s32[64]{0:T(128)} %select_reduce_fusion.1.src_ref, s32[128]{0:T(128)} %get-tuple-element.15.slot_ref, s32[1]{0:T(128)} %bitcast.3.live_ref, bf16[1024,128]{1,0:T(8,128)(2,1)} %get-tuple-element.8.q_ref, bf16[2,256,16,128]{3,2,1,0:T(8,128)(2,1)} %get-tuple-element.9.kv_ref, bf16[512,2048]{1,0:T(8,128)(2,1)} %bitcast.12, ...), custom_call_target="tpu_custom_call" | custom-call | tf_op jit(solution)/shard_map/attend/pallas_call | solution.py:432
  150.9 1.7 %copy.6 = bf16[1,64,2048]{2,1,0:T(8,128)(2,1)} copy(bf16[1,64,2048]{2,1,0:T(8,128)(2,1)} %bitcast.13) | data formatting | bytes 524288

commit v2 on v1

--- a/solution.py
+++ b/solution.py
@@ -31,7 +31,7 @@
 def project_kernel(
     src_ref, hid_ref, w_ref,
     q_ref, kv_ref, res_ref,
-    xg, wv, y, yc, sbuf, rbuf,
+    xg, wr, wf, wv, xs, yc, sbuf, rbuf,
     local_sem, z_send, z_recv, x_send, x_recv, c_send, c_recv, own_sem,
     rs_send, rs_recv, g_send, g_recv, f_send, f_recv,
 ):
@@ -54,7 +54,7 @@
 
     hid_copy = pltpu.make_async_copy(hid_ref, own_rows(c), local_sem.at[0])
     hid_copy.start()
-    w_copy = pltpu.make_async_copy(w_ref, wv, local_sem.at[1])
+    w_copy = pltpu.make_async_copy(w_ref, wr, local_sem.at[1])
     w_copy.start()
     greet(zdev + xdev + ydev + [cdev])
     hid_copy.wait()
@@ -72,22 +72,20 @@
             send(reg, reg, z_send.at[way, 0, s], z_recv.at[way, 0, s], zdev[way])
     send(own_rows(c), own_rows(c), own_sem.at[0], own_sem.at[1], cdev)
 
-    def multiply(zz):
-        units = pl.ds(zz * 16, 16)
-
-        def step(j, carry):
-            cols = pl.ds(pl.multiple_of(j * 256, 256), 256)
-            value = jnp.dot(
-                xg[units].reshape(256, 2048), wv[:, cols], preferred_element_type=jnp.float32
-            )
-            y[units, :, cols] = value.astype(jnp.bfloat16).reshape(16, UNIT, 256)
+    def lay_out(first, count):
+        def step(i, carry):
+            at = pl.multiple_of((first + i) * 32, 32)
+            wf[...] = wr[pl.ds(pl.multiple_of(at * 12, 384), 384), :].astype(jnp.float32)
+            for kind in range(3):
+                for h in range(4):
+                    rows = wf[pl.ds(kind * 4 + h, 32, stride=12), :]
+                    wv[kind, pl.ds(at, 32), h * 128:(h + 1) * 128] = rows.astype(jnp.bfloat16)
             return carry
 
-        lax.fori_loop(0, 6, step, 0)
+        lax.fori_loop(0, count, step, 0)
 
     w_copy.wait()
-    remote(own_rows(1 - c), own_rows(1 - c), own_sem.at[0], own_sem.at[1], cdev).wait_recv()
-    multiply(z)
+    lay_out(0, 8)
 
     events = []
     for d in range(1, 5):
@@ -102,13 +100,12 @@
         remote(reg, reg, x_send.at[way, d - 1, s], x_recv.at[way, d - 1, s], xdev[s]).wait_recv()
         send(reg, reg, c_send.at[way, d - 1, s, 1], c_recv.at[way, d - 1, s, 1], cdev)
 
-    def from_core(way, d):
-        for s in range(2):
-            w = s if d == 4 else way
-            for o in range(2):
-                hh = half if o == 0 else 1 - half
-                reg = region(block_at(way, d), 1 - c, hh, s)
-                remote(reg, reg, c_send.at[w, d - 1, s, o], c_recv.at[w, d - 1, s, o], cdev).wait_recv()
+    def from_core(ev):
+        way, d, s = ev
+        for o in range(2):
+            hh = half if o == 0 else 1 - half
+            reg = region(block_at(way, d), 1 - c, hh, s)
+            remote(reg, reg, c_send.at[way, d - 1, s, o], c_recv.at[way, d - 1, s, o], cdev).wait_recv()
 
     for k, ev in enumerate(events):
         way, d, s = ev
@@ -118,36 +115,34 @@
             send(reg, reg, z_send.at[way, d, s], z_recv.at[way, d, s], zdev[way])
         send(reg, reg, x_send.at[way, d - 1, s], x_recv.at[way, d - 1, s], xdev[s])
         send(reg, reg, c_send.at[way, d - 1, s, 0], c_recv.at[way, d - 1, s, 0], cdev)
-        if k >= 2:
-            from_x(events[k - 2])
-        if k in (5, 9):
-            from_core(0, k // 4)
-            multiply(block_at(0, k // 4))
-        if k in (7, 11):
-            from_core(1, k // 4)
-            multiply(block_at(1, k // 4))
-    from_x(events[-2])
-    from_x(events[-1])
-    for way in range(2):
-        from_core(way, 3)
-        multiply(block_at(way, 3))
-    from_core(0, 4)
-    multiply(block_at(0, 4))
-
+        if k >= 4:
+            from_x(events[k - 4])
+        lay_out(8 + k * 4, 4)
+    for ev in events[-4:]:
+        from_x(ev)
+    remote(own_rows(1 - c), own_rows(1 - c), own_sem.at[0], own_sem.at[1], cdev).wait_recv()
+    for ev in events:
+        from_core(ev)
+
+    def compact(i, carry):
+        xs[pl.ds(pl.multiple_of(i * UNIT, UNIT), UNIT), :] = xg[src_ref[i]]
+        return carry
+
+    lax.fori_loop(0, 64, compact, 0)
     t = z * 2 + c
-    for i in range(4):
-        res_ref[i * UNIT:(i + 1) * UNIT, :] = xg[src_ref[t * 4 + i]]
-
-    def compact(i, carry):
-        to = pl.ds(pl.multiple_of(i * UNIT, UNIT), UNIT)
-        rows = y[src_ref[i]]
-        for j in range(12):
-            yc[j, to, :] = rows[:, j * 128:(j + 1) * 128]
-        return carry
-
-    lax.fori_loop(0, 64, compact, 0)
-
-    kinds = (1, 2, 0)
+    res_ref[...] = xs[pl.ds(pl.multiple_of(t * 64, 64), 64), :]
+
+    def multiply(kind):
+        for way in range(2):
+            rows = slice(way * 512, way * 512 + 512)
+            for n in range(2):
+                value = jnp.dot(
+                    xs[rows, :], wv[kind, :, n * 256:(n + 1) * 256],
+                    preferred_element_type=jnp.float32,
+                ).astype(jnp.bfloat16)
+                yc[kind * 4 + n * 2, rows, :] = value[:, :128]
+                yc[kind * 4 + n * 2 + 1, rows, :] = value[:, 128:]
+
     turn = (1, 3)
 
     def rows_of(way, sub):
@@ -165,67 +160,82 @@
             rs_send.at[way, kind, sub, step], rs_recv.at[way, kind, sub, step], ydev[way],
         ).wait_recv()
 
-    def hop(kind, step):
-        for sub in range(2):
-            for way in range(2):
-                dest = lax.rem(yp + 4 * 3 - turn[way] * (step + 1), 4)
-                if step == 0:
-                    src = yc.at[kind * 4 + dest, rows_of(way, sub), :]
-                else:
-                    arrived(kind, way, sub, step - 1)
-                    sbuf[way, kind, sub, step - 1] = add(kind, dest, way, sub, step - 1)
-                    src = sbuf.at[way, kind, sub, step - 1]
-                send(
-                    src, rbuf.at[way, kind, sub, step],
-                    rs_send.at[way, kind, sub, step], rs_recv.at[way, kind, sub, step], ydev[way],
-                )
+    def hop(kind, step, sub):
+        for way in range(2):
+            dest = lax.rem(yp + 4 * 3 - turn[way] * (step + 1), 4)
+            if step == 0:
+                src = yc.at[kind * 4 + dest, rows_of(way, sub), :]
+            else:
+                arrived(kind, way, sub, step - 1)
+                sbuf[way, kind, sub, step - 1] = add(kind, dest, way, sub, step - 1)
+                src = sbuf.at[way, kind, sub, step - 1]
+            send(
+                src, rbuf.at[way, kind, sub, step],
+                rs_send.at[way, kind, sub, step], rs_recv.at[way, kind, sub, step], ydev[way],
+            )
 
     def kv_rows(section, kind, way, sub):
         return kv_ref.at[kind - 1, pl.ds(section * 64 + way * 32 + sub * 16, 16)]
 
-    def final(kind):
-        for sub in range(2):
-            for way in range(2):
-                arrived(kind, way, sub, 2)
-                value = add(kind, yp, way, sub, 2)
-                if kind == 0:
-                    q_ref[rows_of(way, sub), :] = value
-                else:
-                    reg = kv_rows(xm, kind, way, sub)
-                    reg[...] = value.reshape(16, UNIT, 128)
-                    for o in range(2):
-                        send(
-                            reg, reg, g_send.at[o, kind - 1, way, sub],
-                            g_recv.at[o, kind - 1, way, sub], xdev[o],
-                        )
-
-    def spread(kind):
-        for sub in range(2):
-            for way in range(2):
-                reg = kv_rows(lax.rem(xm + (3, 1)[way], 4), kind, way, sub)
-                remote(
-                    reg, reg, g_send.at[way, kind - 1, way, sub],
-                    g_recv.at[way, kind - 1, way, sub], xdev[way],
-                ).wait_recv()
-                send(
-                    reg, reg, f_send.at[kind - 1, way, sub],
-                    f_recv.at[kind - 1, way, sub], xdev[way],
-                )
-
-    hop(1, 0)
-    hop(1, 1)
-    hop(1, 2)
-    hop(2, 0)
-    final(1)
-    hop(2, 1)
-    hop(2, 2)
-    hop(0, 0)
-    final(2)
-    spread(1)
-    hop(0, 1)
-    hop(0, 2)
-    spread(2)
-    final(0)
+    def final(kind, sub):
+        for way in range(2):
+            arrived(kind, way, sub, 2)
+            value = add(kind, yp, way, sub, 2)
+            if kind == 0:
+                q_ref[rows_of(way, sub), :] = value
+            else:
+                reg = kv_rows(xm, kind, way, sub)
+                reg[...] = value.reshape(16, UNIT, 128)
+                for o in range(2):
+                    send(
+                        reg, reg, g_send.at[o, kind - 1, way, sub],
+                        g_recv.at[o, kind - 1, way, sub], xdev[o],
+                    )
+
+    def spread(kind, sub):
+        for way in range(2):
+            reg = kv_rows(lax.rem(xm + (3, 1)[way], 4), kind, way, sub)
+            remote(
+                reg, reg, g_send.at[way, kind - 1, way, sub],
+                g_recv.at[way, kind - 1, way, sub], xdev[way],
+            ).wait_recv()
+            send(
+                reg, reg, f_send.at[kind - 1, way, sub],
+                f_recv.at[kind - 1, way, sub], xdev[way],
+            )
+
+    K, V, Q = 1, 2, 0
+    multiply(K)
+    hop(K, 0, 0)
+    hop(K, 0, 1)
+    multiply(V)
+    hop(V, 0, 0)
+    multiply(Q)
+    hop(K, 1, 0)
+    hop(K, 1, 1)
+    hop(V, 0, 1)
+    hop(K, 2, 0)
+    hop(K, 2, 1)
+    hop(V, 1, 0)
+    hop(V, 1, 1)
+    final(K, 0)
+    hop(Q, 0, 0)
+    final(K, 1)
+    hop(V, 2, 0)
+    hop(V, 2, 1)
+    spread(K, 0)
+    hop(Q, 0, 1)
+    hop(Q, 1, 0)
+    final(V, 0)
+    spread(K, 1)
+    final(V, 1)
+    hop(Q, 1, 1)
+    hop(Q, 2, 0)
+    hop(Q, 2, 1)
+    spread(V, 0)
+    spread(V, 1)
+    final(Q, 0)
+    final(Q, 1)
     for kind in (1, 2):
         for sub in range(2):
             for way in range(2):
@@ -392,7 +402,7 @@
 
 def local(hidden_in, spans, w_qkv, w_out):
     src, slot, live = plan(spans)
-    w = w_qkv[0].reshape(2048, 1536)
+    w = w_qkv.reshape(24576, 128)
     wo = w_out.reshape(512, 2048)
     bf = jnp.bfloat16
     dma = pltpu.SemaphoreType.DMA
@@ -410,8 +420,10 @@
         out_specs=(vmem, vmem, vmem),
         scratch_shapes=[
             pltpu.VMEM((128, UNIT, 2048), bf),
-            pltpu.VMEM((2048, 1536), bf),
-            pltpu.VMEM((128, UNIT, 1536), bf),
+            pltpu.VMEM((24576, 128), bf),
+            pltpu.VMEM((384, 128), jnp.float32),
+            pltpu.VMEM((3, 2048, 512), bf),
+            pltpu.VMEM((1024, 2048), bf),
             pltpu.VMEM((12, 1024, 128), bf),
             pltpu.VMEM((2, 3, 2, 2, 256, 128), bf),
             pltpu.VMEM((2, 3, 2, 3, 256, 128), bf),

time: 153 us -> 126 us (0.82)
  Pallas kernels: 136 us -> 120 us
  local copies, waits for them, and re-layouts: 13.4 us -> 2.43 us
    pallas_call x1, Pallas kernels: 90.7 us -> 78.6 us  [local(): pl.pallas_call(project_kernel, out_shape=(jax.ShapeDtypeStruct((1024, 128...]
    another operation x1 -> x0, local copies, waits for them, and re-layouts: 11 us -> none  [local(): w = w_qkv[0].reshape(2048, 1536)]
    pallas_call x1, Pallas kernels: 45.4 us -> 41.3 us  [local(): pl.pallas_call(attend_kernel, out_shape=jax.ShapeDtypeStruct((64, 2048),...]
where the time goes in v2:
time: 126 us; the launch traced here: 125 us
  Pallas kernels  120 us (95%)
  other arithmetic  2.95 us (2%)
  local copies, waits for them, and re-layouts  2.43 us (2%)
    pallas_call x1, Pallas kernels, local(): pl.pallas_call(project_kernel, out_shape=(jax.ShapeDtypeStruct((1024, 128...  78.6 us
    pallas_call x1, Pallas kernels, local(): pl.pallas_call(attend_kernel, out_shape=jax.ShapeDtypeStruct((64, 2048),...  41.3 us

profile of v2, /device:TPU:1, one launch (start us, length us, event | category | flops | bytes accessed | tf_op | source)
XLA Modules:
  0.0 125.3 jit_solution(5768439343598165831)
XLA Ops:
  0.0 0.8 slice_bitcast_fusion.1
  0.8 0.8 bitcast_add_fusion
  1.5 0.2 select_reduce_fusion
  1.7 0.2 convert_reduce_fusion
  1.9 1.2 convert_reduce_fusion.1
  3.1 0.6 select_reduce_fusion.1.src_ref
  3.7 78.6 %project.1 = (bf16[1024,128]{1,0:T(8,128)(2,1)}, bf16[2,256,16,128]{3,2,1,0:T(8,128)(2,1)}, bf16[64,2048]{1,0:T(8,128)(2,1)}) custom-call(s32[64]{0:T(128)} %select_reduce_fusion.1.src_ref, bf16[8,16,2048]{2,1,0:T(8,128)(2,1)} %bitcast.16, bf16[24576,128]{1,0:T(8,128)(2,1)} %bitcast.13), custom_call_target="tpu_custom_call" | custom-call | tf_op jit(solution)/shard_map/project/pallas_call | solution.py:412
  82.3 41.3 %attend.1 = bf16[64,2048]{1,0:T(8,128)(2,1)} custom-call(s32[64]{0:T(128)} %select_reduce_fusion.1.src_ref, s32[128]{0:T(128)} %get-tuple-element.15.slot_ref, s32[1]{0:T(128)} %bitcast.3.live_ref, bf16[1024,128]{1,0:T(8,128)(2,1)} %get-tuple-element.8.q_ref, bf16[2,256,16,128]{3,2,1,0:T(8,128)(2,1)} %get-tuple-element.9.kv_ref, bf16[512,2048]{1,0:T(8,128)(2,1)} %bitcast.14, ...), custom_call_target="tpu_custom_call" | custom-call | tf_op jit(solution)/shard_map/attend/pallas_call | solution.py:444
  123.7 1.7 %copy.6 = bf16[1,64,2048]{2,1,0:T(8,128)(2,1)} copy(bf16[1,64,2048]{2,1,0:T(8,128)(2,1)} %bitcast.15) | data formatting | bytes 524288

commit v3 on v2

v3 whole, which is shorter than its diff:
```python
import jax
import jax.numpy as jnp
from jax import lax
from jax.experimental import pallas as pl
from jax.experimental.pallas import tpu as pltpu
from jax.sharding import PartitionSpec as P

MESH = pl.DeviceIdType.MESH
UNIT = 16
NEG = -1e30


def remote(src, dst, send, recv, dev):
    return pltpu.make_async_remote_copy(
        src_ref=src, dst_ref=dst, send_sem=send, recv_sem=recv, device_id=dev, device_id_type=MESH
    )


def greet(devs):
    barrier = pltpu.get_barrier_semaphore()
    for dev in devs:
        pl.semaphore_signal(barrier, inc=1, device_id=dev, device_id_type=MESH)
    pl.semaphore_wait(barrier, len(devs))


def where_am_i():
    t = lax.axis_index("tok")
    return lax.axis_index("mod"), lax.div(t, 2), lax.rem(t, 2), lax.axis_index("tp")


SUBS = 4
PIECE = 1024 // SUBS
ROWS = 512 // SUBS


def make_plan(spans_ref, planv, me):
    down = lax.broadcasted_iota(jnp.int32, (128, 128), 0)
    across = lax.broadcasted_iota(jnp.int32, (128, 128), 1)
    eye = down == across

    def column(row):
        return jnp.sum(jnp.where(eye, row, 0), axis=1, keepdims=True)

    start = spans_ref[0:1, :]
    first = column(start)
    end = column(start + spans_ref[1:2, :])
    kind = column(spans_ref[2:3, :])
    at = across * UNIT
    inside = (at >= first) & (at < end)
    unit_mod = jnp.sum(jnp.where(inside, kind, 0), axis=0, keepdims=True)
    mod_col = column(unit_mod)
    before = (mod_col == unit_mod) & (down < across)
    rank = jnp.sum(jnp.where(before, 1, 0), axis=0, keepdims=True)
    mine = (mod_col == me) & (column(rank) == across)
    planv[0:1, :] = unit_mod * 64 + rank
    planv[1:2, :] = jnp.sum(jnp.where(mine, down, 0), axis=0, keepdims=True)
    live = jnp.sum(jnp.where(unit_mod == me, 1, 0), axis=1, keepdims=True)
    planv[2:3, :] = jnp.broadcast_to(live, (1, 128))


def block_kernel(
    spans_ref, hid_ref, w_ref, wo_ref,
    out_ref,
    planv, plans, xg, wr, wf, wv, wo, xs, yc, sbuf, rbuf, qs, kv,
    kt, vt, heads, zown, csend, crecv, rsend, rrecv,
    local_sem, z_send, z_recv, x_send, x_recv, c_send, c_recv, own_sem,
    rs_send, rs_recv, g_send, g_recv, f_send, f_recv,
    h_send, h_recv, p_send, p_recv, r_send, r_recv,
):
    xm, z, c, yp = where_am_i()
    t = z * 2 + c
    half = lax.rem(xm, 2)
    zdev = [{"tok": lax.rem(z + 1, 8) * 2 + c}, {"tok": lax.rem(z + 7, 8) * 2 + c}]
    xdev = [{"mod": lax.rem(xm + 1, 4)}, {"mod": lax.rem(xm + 3, 4)}]
    ydev = [{"tp": lax.rem(yp + 1, 4)}, {"tp": lax.rem(yp + 3, 4)}]
    opposite = {"tp": lax.rem(yp + 2, 4)}
    cdev = {"tok": z * 2 + 1 - c}

    def region(zz, cc, hh, s):
        units = pl.ds((zz * 2 + cc) * 8, 8)
        return xg.at[units, :, pl.ds(pl.multiple_of(hh * 1024 + s * PIECE, PIECE), PIECE)]

    def own_rows(cc):
        return xg.at[pl.ds((z * 2 + cc) * 8, 8)]

    def block_at(way, d):
        return lax.rem(z + 8 - d, 8) if way == 0 else lax.rem(z + d, 8)

    hid_copy = pltpu.make_async_copy(hid_ref, own_rows(c), local_sem.at[0])
    hid_copy.start()
    w_copy = pltpu.make_async_copy(w_ref, wr, local_sem.at[1])
    w_copy.start()
    wo_copy = pltpu.make_async_copy(wo_ref, wo, local_sem.at[2])
    wo_copy.start()
    greet(zdev + xdev + ydev + [opposite, cdev])
    hid_copy.wait()

    sent = []

    def send(src, dst, ssem, rsem, dev):
        copy = remote(src, dst, ssem, rsem, dev)
        copy.start()
        sent.append(copy)

    for s in range(SUBS):
        for way in range(2):
            reg = region(z, c, half, s)
            send(reg, reg, z_send.at[way, 0, s], z_recv.at[way, 0, s], zdev[way])
    send(own_rows(c), own_rows(c), own_sem.at[0], own_sem.at[1], cdev)

    make_plan(spans_ref, planv, xm)
    plan_copy = pltpu.make_async_copy(planv, plans, local_sem.at[3])
    plan_copy.start()

    def lay_out(first, count):
        def step(i, carry):
            at = pl.multiple_of((first + i) * 32, 32)
            wf[...] = wr[pl.ds(pl.multiple_of(at * 12, 384), 384), :].astype(jnp.float32)
            for j in range(12):
                rows = wf[pl.ds(j, 32, stride=12), :]
                wv[j, pl.ds(at, 32), :] = rows.astype(jnp.bfloat16)
            return carry

        lax.fori_loop(0, count, step, 0)

    events = []
    for d in range(1, 5):
        for s in range(SUBS):
            for way in range(2):
                if d < 4 or s // (SUBS // 2) == way:
                    events.append((way, d, s))
    events[-SUBS:] = [(s // (SUBS // 2), 4, s) for k in range(SUBS // 2) for s in (k, k + SUBS // 2)]

    def from_x(ev):
        way, d, s = ev
        reg = region(block_at(way, d), c, 1 - half, s)
        remote(reg, reg, x_send.at[way, d - 1, s], x_recv.at[way, d - 1, s], xdev[s % 2]).wait_recv()
        send(reg, reg, c_send.at[way, d - 1, s, 1], c_recv.at[way, d - 1, s, 1], cdev)

    def from_core(ev):
        way, d, s = ev
        for o in range(2):
            hh = half if o == 0 else 1 - half
            reg = region(block_at(way, d), 1 - c, hh, s)
            remote(reg, reg, c_send.at[way, d - 1, s, o], c_recv.at[way, d - 1, s, o], cdev).wait_recv()

    w_copy.wait()
    lay_out(0, 8)
    lag = 2 * SUBS
    laid = 8
    for k, ev in enumerate(events):
        way, d, s = ev
        reg = region(block_at(way, d), c, half, s)
        remote(reg, reg, z_send.at[way, d - 1, s], z_recv.at[way, d - 1, s], zdev[way]).wait_recv()
        if d < 3 or (d == 3 and s // (SUBS // 2) == way):
            send(reg, reg, z_send.at[way, d, s], z_recv.at[way, d, s], zdev[way])
        send(reg, reg, x_send.at[way, d - 1, s], x_recv.at[way, d - 1, s], xdev[s % 2])
        send(reg, reg, c_send.at[way, d - 1, s, 0], c_recv.at[way, d - 1, s, 0], cdev)
        if k >= lag:
            from_x(events[k - lag])
        upto = 8 + 56 * (k + 1) // len(events)
        if upto > laid:
            lay_out(laid, upto - laid)
            laid = upto
    for ev in events[-lag:]:
        from_x(ev)
    remote(own_rows(1 - c), own_rows(1 - c), own_sem.at[0], own_sem.at[1], cdev).wait_recv()
    for ev in events:
        from_core(ev)

    plan_copy.wait()

    def compact(i, carry):
        xs[pl.ds(pl.multiple_of(i * UNIT, UNIT), UNIT), :] = xg[plans[1, i]]
        return carry

    lax.fori_loop(0, 64, compact, 0)

    turn = (1, 3)

    def dest_of(way, step):
        return lax.rem(yp + 12 - turn[way] * (step + 1), 4)

    def multiply(kind, part):
        for way in range(2):
            rows = slice(way * 512, way * 512 + 512)
            pair = [kind * 4 + dest_of(way, 2 * part + k) for k in range(2)]
            weights = jnp.concatenate([wv[j] for j in pair], axis=1)
            value = jnp.dot(xs[rows, :], weights, preferred_element_type=jnp.float32).astype(jnp.bfloat16)
            yc[pair[0], rows, :] = value[:, :128]
            yc[pair[1], rows, :] = value[:, 128:]

    def rows_of(way, sub):
        return pl.ds(way * 512 + sub * ROWS, ROWS)

    def add(kind, dest, way, sub, step):
        return (
            yc[kind * 4 + dest, rows_of(way, sub), :].astype(jnp.float32)
            + rbuf[way, kind, sub, step].astype(jnp.float32)
        ).astype(jnp.bfloat16)

    def arrived(kind, way, sub, step):
        remote(
            rbuf.at[way, kind, sub, step], rbuf.at[way, kind, sub, step],
            rs_send.at[way, kind, sub, step], rs_recv.at[way, kind, sub, step], ydev[way],
        ).wait_recv()

    def halves(group):
        return range(group * SUBS // 2, (group + 1) * SUBS // 2)

    def hop(kind, step, group):
        for sub in halves(group):
            for way in range(2):
                dest = dest_of(way, step)
                if step == 0:
                    src = yc.at[kind * 4 + dest, rows_of(way, sub), :]
                else:
                    arrived(kind, way, sub, step - 1)
                    sbuf[way, kind, sub, step - 1] = add(kind, dest, way, sub, step - 1)
                    src = sbuf.at[way, kind, sub, step - 1]
                send(
                    src, rbuf.at[way, kind, sub, step],
                    rs_send.at[way, kind, sub, step], rs_recv.at[way, kind, sub, step], ydev[way],
                )

    def kv_rows(section, kind, way, sub):
        units = ROWS // UNIT
        return kv.at[kind - 1, pl.ds(section * 64 + way * 32 + sub * units, units)]

    def final(kind, group):
        for sub in halves(group):
            for way in range(2):
                arrived(kind, way, sub, 2)
                value = add(kind, yp, way, sub, 2)
                if kind == 0:
                    qs[rows_of(way, sub), :] = value
                else:
                    reg = kv_rows(xm, kind, way, sub)
                    reg[...] = value.reshape(ROWS // UNIT, UNIT, 128)
                    for o in range(2):
                        send(
                            reg, reg, g_send.at[o, kind - 1, way, sub],
                            g_recv.at[o, kind - 1, way, sub], xdev[o],
                        )

    def spread(kind, group):
        for sub in halves(group):
            for way in range(2):
                reg = kv_rows(lax.rem(xm + (3, 1)[way], 4), kind, way, sub)
                remote(
                    reg, reg, g_send.at[way, kind - 1, way, sub],
                    g_recv.at[way, kind - 1, way, sub], xdev[way],
                ).wait_recv()
                send(
                    reg, reg, f_send.at[kind - 1, way, sub],
                    f_recv.at[kind - 1, way, sub], xdev[way],
                )

    K, V, Q = 1, 2, 0
    multiply(K, 0)
    hop(K, 0, 0)
    hop(K, 0, 1)
    multiply(V, 0)
    hop(V, 0, 0)
    multiply(K, 1)
    hop(K, 1, 0)
    hop(K, 1, 1)
    hop(V, 0, 1)
    multiply(V, 1)
    hop(K, 2, 0)
    hop(K, 2, 1)
    multiply(Q, 0)
    hop(V, 1, 0)
    hop(V, 1, 1)
    final(K, 0)
    hop(Q, 0, 0)
    final(K, 1)
    multiply(Q, 1)
    hop(V, 2, 0)
    hop(V, 2, 1)
    spread(K, 0)
    hop(Q, 0, 1)
    hop(Q, 1, 0)
    final(V, 0)
    spread(K, 1)
    final(V, 1)
    hop(Q, 1, 1)
    hop(Q, 2, 0)
    hop(Q, 2, 1)
    spread(V, 0)
    spread(V, 1)
    final(Q, 0)
    final(Q, 1)
    for kind in (1, 2):
        for sub in range(SUBS):
            for way in range(2):
                reg = kv_rows(lax.rem(xm + (1, 3)[way], 4), kind, way, sub)
                remote(
                    reg, reg, g_send.at[1 - way, kind - 1, way, sub],
                    g_recv.at[1 - way, kind - 1, way, sub], xdev[1 - way],
                ).wait_recv()
                reg = kv_rows(lax.rem(xm + 2, 4), kind, way, sub)
                remote(
                    reg, reg, f_send.at[kind - 1, way, sub],
                    f_recv.at[kind - 1, way, sub], xdev[way],
                ).wait_recv()

    def order_keys(u, carry):
        to = pl.ds(pl.multiple_of(u * UNIT, UNIT), UNIT)
        unit = plans[0, u]
        kt[to, :] = kv[0, unit]
        vt[to, :] = kv[1, unit]
        return carry

    lax.fori_loop(0, 128, order_keys, 0)

    dests = [lax.rem(z + k, 8) for k in (4, 3, 5, 2, 6, 1, 7, 0)]
    hdev = [ydev[0], opposite, ydev[1]]

    def my_cols(p):
        return pl.ds(pl.multiple_of(p * 128, 128), 128)

    def attend(i):
        d = dests[i]
        query = qs[pl.ds(pl.multiple_of(d * 128, 128), 128), :]
        scores = lax.dot_general(
            query, kt[...], (((1,), (1,)), ((), ())), preferred_element_type=jnp.float32
        ) * (128 ** -0.5)
        base = jnp.concatenate(
            [jnp.full((UNIT, 1), plans[1, d * 8 + k] * UNIT, jnp.int32) for k in range(8)], axis=0
        )
        row = lax.broadcasted_iota(jnp.int32, (128, 1), 0)
        pos = base + lax.rem(row, UNIT)
        key = lax.broadcasted_iota(jnp.int32, (128, 2048), 1)
        scores = jnp.where(key <= pos, scores, NEG)
        top = jnp.max(scores, axis=1, keepdims=True)
        weights = jnp.exp(scores - top)
        total = jnp.sum(weights, axis=1, keepdims=True)
        mixed = jnp.dot(weights.astype(jnp.bfloat16), vt[...], preferred_element_type=jnp.float32)
        heads[i, :, my_cols(yp)] = (mixed / total).astype(jnp.bfloat16)
        mine = heads.at[i, :, my_cols(yp)]
        for k in range(3):
            send(mine, mine, h_send.at[i, k], h_recv.at[i, k], hdev[k])

    def project(i):
        for k in range(3):
            other = heads.at[i, :, my_cols(lax.rem(yp + 3 - k, 4))]
            remote(other, other, h_send.at[i, k], h_recv.at[i, k], hdev[k]).wait_recv()

        def part(j, carry):
            cols = pl.ds(pl.multiple_of(j * 512, 512), 512)
            value = jnp.dot(heads[i], wo[:, cols], preferred_element_type=jnp.float32)
            first = value[:64]
            second = value[64:]
            zown[i, :, cols] = jnp.where(c == 0, first, second)
            csend[i, :, cols] = jnp.where(c == 0, second, first).astype(jnp.bfloat16)
            return carry

        lax.fori_loop(0, 4, part, 0)
        send(csend.at[i], crecv.at[i], p_send.at[i], p_recv.at[i], cdev)

    top_of = {(0, 0): 3, (0, 1): 4, (1, 0): 4, (1, 1): 3}

    def ring(way, dist, part):
        i = {4: 0, 3: 1, 2: 3, 1: 5}[dist] + (1 if way == 1 and dist < 4 else 0)
        cols = slice(part * 1024, part * 1024 + 1024)
        value = zown[i, :, cols] + crecv[i, :, cols].astype(jnp.float32)
        if dist < top_of[(way, part)]:
            came = rrecv.at[way, dist, part]
            remote(
                came, came, r_send.at[way, dist, part], r_recv.at[way, dist, part], zdev[way]
            ).wait_recv()
            value = value + came[...].astype(jnp.float32)
        rsend[way, dist - 1, part] = value.astype(jnp.bfloat16)
        send(
            rsend.at[way, dist - 1, part], rrecv.at[way, dist - 1, part],
            r_send.at[way, dist - 1, part], r_recv.at[way, dist - 1, part], zdev[way],
        )

    def core_sum(i):
        remote(crecv.at[i], crecv.at[i], p_send.at[i], p_recv.at[i], cdev).wait_recv()

    attend(0)
    attend(1)
    wo_copy.wait()
    attend(2)
    project(0)
    attend(3)
    project(1)
    core_sum(0)
    ring(1, 4, 0)
    ring(0, 4, 1)
    attend(4)
    project(2)
    core_sum(1)
    ring(0, 3, 0)
    core_sum(2)
    ring(1, 3, 1)
    attend(5)
    project(3)
    attend(6)
    project(4)
    ring(0, 3, 1)
    ring(1, 3, 0)
    attend(7)
    project(5)
    core_sum(3)
    ring(0, 2, 0)
    core_sum(4)
    ring(1, 2, 1)
    project(6)
    ring(0, 2, 1)
    ring(1, 2, 0)
    project(7)
    core_sum(5)
    ring(0, 1, 0)
    core_sum(6)
    ring(1, 1, 1)
    ring(0, 1, 1)
    ring(1, 1, 0)
    core_sum(7)

    row = lax.broadcasted_iota(jnp.int32, (64, 1), 0) + t * 64
    alive = row < planv[2:3, 0:1] * UNIT
    residual = xs.at[pl.ds(pl.multiple_of(t * 64, 64), 64), :]
    for part in range(2):
        cols = slice(part * 1024, part * 1024 + 1024)
        value = zown[7, :, cols] + crecv[7, :, cols].astype(jnp.float32)
        value = value + residual[:, cols].astype(jnp.float32)
        for way in (part, 1 - part):
            came = rrecv.at[way, 0, part]
            remote(
                came, came, r_send.at[way, 0, part], r_recv.at[way, 0, part], zdev[way]
            ).wait_recv()
            value = value + came[...].astype(jnp.float32)
        out_ref[:, cols] = jnp.where(alive, value, 0.0).astype(jnp.bfloat16)
    for copy in sent:
        copy.wait_send()


def local(hidden_in, spans, w_qkv, w_out):
    bf = jnp.bfloat16
    dma = pltpu.SemaphoreType.DMA
    vmem = pl.BlockSpec(memory_space=pltpu.VMEM)
    anyw = pl.BlockSpec(memory_space=pl.ANY)
    out = pl.pallas_call(
        block_kernel,
        out_shape=jax.ShapeDtypeStruct((64, 2048), bf),
        in_specs=[vmem, anyw, anyw, anyw],
        out_specs=vmem,
        scratch_shapes=[
            pltpu.VMEM((8, 128), jnp.int32),
            pltpu.SMEM((8, 128), jnp.int32),
            pltpu.VMEM((128, UNIT, 2048), bf),
            pltpu.VMEM((24576, 128), bf),
            pltpu.VMEM((384, 128), jnp.float32),
            pltpu.VMEM((12, 2048, 128), bf),
            pltpu.VMEM((512, 2048), bf),
            pltpu.VMEM((1024, 2048), bf),
            pltpu.VMEM((12, 1024, 128), bf),
            pltpu.VMEM((2, 3, SUBS, 2, ROWS, 128), bf),
            pltpu.VMEM((2, 3, SUBS, 3, ROWS, 128), bf),
            pltpu.VMEM((1024, 128), bf),
            pltpu.VMEM((2, 256, UNIT, 128), bf),
            pltpu.VMEM((2048, 128), bf),
            pltpu.VMEM((2048, 128), bf),
            pltpu.VMEM((8, 128, 512), bf),
            pltpu.VMEM((8, 64, 2048), jnp.float32),
            pltpu.VMEM((8, 64, 2048), bf),
            pltpu.VMEM((8, 64, 2048), bf),
            pltpu.VMEM((2, 4, 2, 64, 1024), bf),
            pltpu.VMEM((2, 4, 2, 64, 1024), bf),
            dma((4,)),
            dma((2, 4, SUBS)), dma((2, 4, SUBS)),
            dma((2, 4, SUBS)), dma((2, 4, SUBS)),
            dma((2, 4, SUBS, 2)), dma((2, 4, SUBS, 2)),
            dma((2,)),
            dma((2, 3, SUBS, 3)), dma((2, 3, SUBS, 3)),
            dma((2, 2, 2, SUBS)), dma((2, 2, 2, SUBS)),
            dma((2, 2, SUBS)), dma((2, 2, SUBS)),
            dma((8, 3)), dma((8, 3)),
            dma((8,)), dma((8,)),
            dma((2, 4, 2)), dma((2, 4, 2)),
        ],
        compiler_params=pltpu.CompilerParams(
            collective_id=1, has_side_effects=True, vmem_limit_bytes=60 * 1024 * 1024
        ),
        name="block",
    )(
        spans.T, hidden_in.reshape(8, UNIT, 2048), w_qkv.reshape(24576, 128), w_out.reshape(512, 2048)
    )
    return out[None]


def solution(mesh):
    in_specs = (P("tok", "tp"), P(), P("mod", "tp", None, "tok", None), P("mod", "tok", None, "tp"))
    out_specs = P("mod", "tok", "tp")
    return jax.shard_map(local, mesh=mesh, in_specs=in_specs, out_specs=out_specs, check_vma=False)
```

time: 126 us -> 112 us (0.89)
  Pallas kernels: 120 us -> 110 us
  other arithmetic: 2.95 us -> 0 us
    pallas_call x2 -> x1, Pallas kernels: 120 us -> 110 us  [local(): pl.pallas_call(block_kernel, out_shape=jax.ShapeDtypeStruct((64, 2048), b...]
    reduce_sum x4 -> x0, other arithmetic: 2.19 us -> none  [the longest x1 1.22 us: plan(): live = jnp.sum(mine.astype(jnp.int32)).reshape(1)]
where the time goes in v3:
time: 112 us
  Pallas kernels  110 us (98%)
  local copies, waits for them, and re-layouts  1.67 us (1%)
    pallas_call x1, Pallas kernels, local(): pl.pallas_call(block_kernel, out_shape=jax.ShapeDtypeStruct((64, 2048), b...  110 us

profile of v3, /device:TPU:1, one launch (start us, length us, event | category | flops | bytes accessed | tf_op | source)
XLA Modules:
  0.0 112.0 jit_solution(12670860075250288335)
XLA Ops:
  0.0 110.4 %block.1 = bf16[64,2048]{1,0:T(8,128)(2,1)} custom-call(s32[3,128]{1,0:T(4,128)} %bitcast.9, bf16[8,16,2048]{2,1,0:T(8,128)(2,1)} %bitcast.8, bf16[24576,128]{1,0:T(8,128)(2,1)} %bitcast.5, bf16[512,2048]{1,0:T(8,128)(2,1)} %bitcast.6), custom_call_target="tpu_custom_call" | custom-call | tf_op jit(solution)/shard_map/block/pallas_call | solution.py:446
  110.4 1.7 %copy.6 = bf16[1,64,2048]{2,1,0:T(8,128)(2,1)} copy(bf16[1,64,2048]{2,1,0:T(8,128)(2,1)} %bitcast.7) | data formatting | bytes 524288

commit v4 on v3

v4 whole, which is shorter than its diff:
```python
import jax
import jax.numpy as jnp
from jax import lax
from jax.experimental import pallas as pl
from jax.experimental.pallas import tpu as pltpu
from jax.sharding import PartitionSpec as P

MESH = pl.DeviceIdType.MESH
UNIT = 16
NEG = -1e30


def remote(src, dst, send, recv, dev):
    return pltpu.make_async_remote_copy(
        src_ref=src, dst_ref=dst, send_sem=send, recv_sem=recv, device_id=dev, device_id_type=MESH
    )


def greet(devs):
    barrier = pltpu.get_barrier_semaphore()
    for dev in devs:
        pl.semaphore_signal(barrier, inc=1, device_id=dev, device_id_type=MESH)
    pl.semaphore_wait(barrier, len(devs))


def where_am_i():
    t = lax.axis_index("tok")
    return lax.axis_index("mod"), lax.div(t, 2), lax.rem(t, 2), lax.axis_index("tp")


STAGGER = 10
SUBS = 4
PIECE = 1024 // SUBS
GROUPS = 2
ROWS = 512 // GROUPS


def make_plan(spans_ref, planv, me):
    down = lax.broadcasted_iota(jnp.int32, (128, 128), 0)
    across = lax.broadcasted_iota(jnp.int32, (128, 128), 1)
    eye = down == across

    def column(row):
        return jnp.sum(jnp.where(eye, row, 0), axis=1, keepdims=True)

    start = spans_ref[0:1, :]
    first = column(start)
    end = column(start + spans_ref[1:2, :])
    kind = column(spans_ref[2:3, :])
    at = across * UNIT
    inside = (at >= first) & (at < end)
    unit_mod = jnp.sum(jnp.where(inside, kind, 0), axis=0, keepdims=True)
    mod_col = column(unit_mod)
    before = (mod_col == unit_mod) & (down < across)
    rank = jnp.sum(jnp.where(before, 1, 0), axis=0, keepdims=True)
    mine = (mod_col == me) & (column(rank) == across)
    planv[0:1, :] = unit_mod * 64 + rank
    planv[1:2, :] = jnp.sum(jnp.where(mine, down, 0), axis=0, keepdims=True)
    live = jnp.sum(jnp.where(unit_mod == me, 1, 0), axis=1, keepdims=True)
    planv[2:3, :] = jnp.broadcast_to(live, (1, 128))


def block_kernel(
    spans_ref, hid_ref, w_ref, wo_ref,
    out_ref,
    planv, plans, xg, wr, wf, wv, wo, xs, yc, sbuf, rbuf, qs, keys, values,
    kt, vt, probs, totals, heads, zown, csend, crecv, rsend, rrecv,
    local_sem, w_sem, sent_sem, z_recv, x_recv, c_recv, rs_recv, g_recv, gf_recv,
    h_recv, p_recv, r_recv,
):
    xm, z, c, yp = where_am_i()
    t = z * 2 + c
    half = lax.rem(xm, 2)
    zdev = [{"tok": lax.rem(z + 1, 8) * 2 + c}, {"tok": lax.rem(z + 7, 8) * 2 + c}]
    xdev = [{"mod": lax.rem(xm + 1, 4)}, {"mod": lax.rem(xm + 3, 4)}]
    ydev = [{"tp": lax.rem(yp + 1, 4)}, {"tp": lax.rem(yp + 3, 4)}]
    opposite = {"tp": lax.rem(yp + 2, 4)}
    cdev = {"tok": z * 2 + 1 - c}

    def region(zz, cc, hh, s):
        return xg.at[hh * SUBS + s, pl.ds((zz * 2 + cc) * 8, 8)]

    def own_rows(cc):
        return xg.at[:, pl.ds((z * 2 + cc) * 8, 8)]

    def block_at(way, d):
        return lax.rem(z + 8 - d, 8) if way == 0 else lax.rem(z + d, 8)

    hid_copies = [
        pltpu.make_async_copy(
            hid_ref.at[:, :, p * PIECE:(p + 1) * PIECE],
            xg.at[p, pl.ds((z * 2 + c) * 8, 8)],
            local_sem.at[0],
        )
        for p in range(2 * SUBS)
    ]
    for copy in hid_copies:
        copy.start()
    w_copies = []
    for k in range(4):
        part = pl.ds(k * 6144, 6144)
        w_copies.append(pltpu.make_async_copy(w_ref.at[part], wr.at[part], w_sem.at[k]))
        w_copies[k].start()
    wo_copy = pltpu.make_async_copy(wo_ref, wo, local_sem.at[2])
    wo_copy.start()
    greet(zdev + xdev + ydev + [opposite, cdev])
    pltpu.make_async_copy(own_rows(c), own_rows(c), local_sem.at[0]).wait()

    def send(src, dst, line, rsem, dev):
        remote(src, dst, sent_sem.at[line], rsem, dev).start()

    def arrive(ref, rsem):
        remote(ref, ref, sent_sem.at[0], rsem, cdev).wait_recv()

    def left(ref, line):
        remote(ref, ref, sent_sem.at[line], c_recv.at[0], cdev).wait_send()

    events = []
    for d in range(1, 5):
        for s in range(SUBS):
            for way in range(2):
                if d < 4 or s // (SUBS // 2) == way:
                    events.append((way, d, s))
    events[-SUBS:] = [(s // (SUBS // 2), 4, s) for k in range(SUBS // 2) for s in (k, k + SUBS // 2)]
    event_at = {ev: k for k, ev in enumerate(events)}

    def lay_out(first, count):
        def step(i, carry):
            at = pl.multiple_of((first + i) * 32, 32)
            wf[...] = wr[pl.ds(pl.multiple_of(at * 12, 384), 384), :].astype(jnp.float32)
            for j in range(12):
                rows = wf[pl.ds(j, 32, stride=12), :]
                wv[j, pl.ds(at, 32), :] = rows.astype(jnp.bfloat16)
            return carry

        lax.fori_loop(0, count, step, 0)

    laid = 0
    for s in range(SUBS):
        for way in range(2):
            reg = region(z, c, half, s)
            send(reg, reg, 0, z_recv.at[event_at[way, 1, s]], zdev[way])
        if s == 0:
            make_plan(spans_ref, planv, xm)
            plan_copy = pltpu.make_async_copy(planv, plans, local_sem.at[3])
            plan_copy.start()
        elif s < SUBS - 1:
            w_copies[s - 1].wait()
            lay_out(laid, STAGGER)
            laid += STAGGER
    send(own_rows(c), own_rows(c), 2, c_recv.at[0], cdev)
    for copy in w_copies[2:]:
        copy.wait()

    def from_x(k):
        way, d, s = events[k]
        reg = region(block_at(way, d), c, 1 - half, s)
        arrive(reg, x_recv.at[k])
        send(reg, reg, 2, c_recv.at[0], cdev)

    lag = 2 * SUBS
    for k, ev in enumerate(events):
        way, d, s = ev
        reg = region(block_at(way, d), c, half, s)
        arrive(reg, z_recv.at[k])
        if d < 3 or (d == 3 and s // (SUBS // 2) == way):
            send(reg, reg, 0, z_recv.at[event_at[way, d + 1, s]], zdev[way])
        send(reg, reg, 1, x_recv.at[k], xdev[s % 2])
        send(reg, reg, 2, c_recv.at[0], cdev)
        if k >= lag:
            from_x(k - lag)
        upto = 2 * STAGGER + (64 - 2 * STAGGER) * (k + 1) // len(events)
        if upto > laid:
            lay_out(laid, upto - laid)
            laid = upto
    for k in range(len(events) - lag, len(events)):
        from_x(k)
    arrive(xg.at[:, 0:64], c_recv.at[0])

    plan_copy.wait()

    def compact(i, carry):
        unit = plans[1, i]
        to = pl.ds(pl.multiple_of(i * UNIT, UNIT), UNIT)
        for p in range(2 * SUBS):
            xs[to, p * PIECE:(p + 1) * PIECE] = xg[p, unit]
        return carry

    lax.fori_loop(0, 64, compact, 0)

    turn = (1, 3)

    def dest_of(way, step):
        return lax.rem(yp + 12 - turn[way] * (step + 1), 4)

    def multiply(kind, part):
        for way in range(2):
            rows = slice(way * 512, way * 512 + 512)
            pair = [kind * 4 + dest_of(way, 2 * part + k) for k in range(2)]
            weights = jnp.concatenate([wv[j] for j in pair], axis=1)
            value = jnp.dot(xs[rows, :], weights, preferred_element_type=jnp.float32).astype(jnp.bfloat16)
            yc[pair[0], rows, :] = value[:, :128]
            yc[pair[1], rows, :] = value[:, 128:]

    def rows_of(way, sub):
        return pl.ds(way * 512 + sub * ROWS, ROWS)

    def add(kind, dest, way, sub, step):
        return (
            yc[kind * 4 + dest, rows_of(way, sub), :].astype(jnp.float32)
            + rbuf[way, kind, sub, step].astype(jnp.float32)
        ).astype(jnp.bfloat16)

    def arrived(kind, way, sub, step):
        arrive(rbuf.at[way, kind, sub, step], rs_recv.at[way, kind, sub, step])

    def hop(kind, step, sub):
        for way in range(2):
            dest = dest_of(way, step)
            if step == 0:
                src = yc.at[kind * 4 + dest, rows_of(way, sub), :]
            else:
                arrived(kind, way, sub, step - 1)
                sbuf[way, kind, sub, step - 1] = add(kind, dest, way, sub, step - 1)
                src = sbuf.at[way, kind, sub, step - 1]
            send(src, rbuf.at[way, kind, sub, step], 3, rs_recv.at[way, kind, sub, step], ydev[way])

    kv = (keys, values)

    def kv_rows(section, kind, way, sub):
        units = ROWS // UNIT
        return kv[kind - 1].at[pl.ds(section * 64 + way * 32 + sub * units, units)]

    def final(kind, sub):
        for way in range(2):
            arrived(kind, way, sub, 2)
            value = add(kind, yp, way, sub, 2)
            if kind == 0:
                qs[rows_of(way, sub), :] = value
            else:
                reg = kv_rows(xm, kind, way, sub)
                reg[...] = value.reshape(ROWS // UNIT, UNIT, 128)
                send(reg, reg, 4, g_recv.at[kind - 1, way, sub], xdev[way])
                send(reg, reg, 4, gf_recv.at[kind - 1], xdev[1 - way])

    def spread(kind, sub):
        for way in range(2):
            reg = kv_rows(lax.rem(xm + (3, 1)[way], 4), kind, way, sub)
            arrive(reg, g_recv.at[kind - 1, way, sub])
            send(reg, reg, 5, gf_recv.at[kind - 1], xdev[way])

    K, V, Q = 1, 2, 0
    multiply(K, 0)
    hop(K, 0, 0)
    hop(K, 0, 1)
    multiply(V, 0)
    hop(V, 0, 0)
    multiply(K, 1)
    hop(K, 1, 0)
    hop(K, 1, 1)
    hop(V, 0, 1)
    multiply(V, 1)
    hop(K, 2, 0)
    hop(K, 2, 1)
    multiply(Q, 0)
    hop(V, 1, 0)
    hop(V, 1, 1)
    final(K, 0)
    hop(Q, 0, 0)
    final(K, 1)
    multiply(Q, 1)
    hop(V, 2, 0)
    hop(V, 2, 1)
    spread(K, 0)
    hop(Q, 0, 1)
    hop(Q, 1, 0)
    final(V, 0)
    spread(K, 1)
    final(V, 1)
    hop(Q, 1, 1)
    hop(Q, 2, 0)
    hop(Q, 2, 1)
    spread(V, 0)
    spread(V, 1)

    def in_token_order(kind, to_ref):
        arrive(kv[kind - 1].at[0:128], gf_recv.at[kind - 1])

        def step(i, carry):
            for k in range(4):
                u = i * 4 + k
                to_ref[pl.ds(pl.multiple_of(u * UNIT, UNIT), UNIT), :] = kv[kind - 1][plans[0, u]]
            return carry

        lax.fori_loop(0, 32, step, 0)

    in_token_order(K, kt)
    final(Q, 0)
    final(Q, 1)

    dests = [lax.rem(z + k, 8) for k in (4, 3, 5, 2, 6, 1, 7, 0)]
    hdev = [ydev[0], opposite, ydev[1]]

    def my_cols(p):
        return pl.ds(pl.multiple_of(p * 128, 128), 128)

    def score(i):
        d = dests[i]
        query = qs[pl.ds(pl.multiple_of(d * 128, 128), 128), :]
        scores = lax.dot_general(
            query, kt[...], (((1,), (1,)), ((), ())), preferred_element_type=jnp.float32
        ) * (128 ** -0.5)
        base = jnp.concatenate(
            [jnp.full((UNIT, 1), plans[1, d * 8 + k] * UNIT, jnp.int32) for k in range(8)], axis=0
        )
        row = lax.broadcasted_iota(jnp.int32, (128, 1), 0)
        pos = base + lax.rem(row, UNIT)
        key = lax.broadcasted_iota(jnp.int32, (128, 2048), 1)
        scores = jnp.where(key <= pos, scores, NEG)
        top = jnp.max(scores, axis=1, keepdims=True)
        weights = jnp.exp(scores - top)
        totals[i] = jnp.sum(weights, axis=1, keepdims=True)
        probs[i] = weights.astype(jnp.bfloat16)

    def mix(i):
        mixed = jnp.dot(probs[i], vt[...], preferred_element_type=jnp.float32)
        heads[i, :, my_cols(yp)] = (mixed / totals[i]).astype(jnp.bfloat16)
        mine = heads.at[i, :, my_cols(yp)]
        for k in range(3):
            send(mine, mine, 6, h_recv.at[i], hdev[k])

    def project(i):
        arrive(heads.at[i, :, 0:384], h_recv.at[i])

        def part(j, carry):
            cols = pl.ds(pl.multiple_of(j * 512, 512), 512)
            value = jnp.dot(heads[i], wo[:, cols], preferred_element_type=jnp.float32)
            first = value[:64]
            second = value[64:]
            zown[i, :, cols] = jnp.where(c == 0, first, second)
            csend[i, :, cols] = jnp.where(c == 0, second, first).astype(jnp.bfloat16)
            return carry

        lax.fori_loop(0, 4, part, 0)
        send(csend.at[i], crecv.at[i], 7, p_recv.at[i], cdev)

    top_of = {(0, 0): 3, (0, 1): 4, (1, 0): 4, (1, 1): 3}

    def number(way, dist, part, q):
        if dist < 4:
            return (((way * 3 + dist - 1) * 2) + part) * 2 + q
        return 24 + way * 2 + q

    def ring(way, dist, part):
        i = {4: 0, 3: 1, 2: 3, 1: 5}[dist] + (1 if way == 1 and dist < 4 else 0)
        for q in range(2):
            cols = slice(part * 1024 + q * 512, part * 1024 + q * 512 + 512)
            value = zown[i, :, cols] + crecv[i, :, cols].astype(jnp.float32)
            if dist < top_of[(way, part)]:
                came = number(way, dist + 1, part, q)
                arrive(rrecv.at[came], r_recv.at[came])
                value = value + rrecv[came].astype(jnp.float32)
            n = number(way, dist, part, q)
            rsend[n] = value.astype(jnp.bfloat16)
            send(rsend.at[n], rrecv.at[n], 8, r_recv.at[n], zdev[way])

    def core_sum(i):
        arrive(crecv.at[i], p_recv.at[i])

    def both(*ops):
        for op in ops:
            ring(*op)

    score(0)
    score(1)
    score(2)
    wo_copy.wait()
    in_token_order(V, vt)
    mix(0)
    mix(1)
    mix(2)
    score(3)
    project(0)
    mix(3)
    project(1)
    core_sum(0)
    both((1, 4, 0), (0, 4, 1))
    project(2)
    score(4)
    mix(4)
    core_sum(1)
    core_sum(2)
    both((0, 3, 0), (1, 3, 1))
    project(3)
    score(5)
    mix(5)
    project(4)
    score(6)
    mix(6)
    both((0, 3, 1), (1, 3, 0))
    project(5)
    score(7)
    mix(7)
    core_sum(3)
    core_sum(4)
    both((0, 2, 0), (1, 2, 1))
    project(6)
    both((0, 2, 1), (1, 2, 0))
    project(7)
    core_sum(5)
    core_sum(6)
    both((0, 1, 0), (1, 1, 1), (0, 1, 1), (1, 1, 0))
    core_sum(7)

    row = lax.broadcasted_iota(jnp.int32, (64, 1), 0) + t * 64
    alive = row < planv[2:3, 0:1] * UNIT
    residual = xs.at[pl.ds(pl.multiple_of(t * 64, 64), 64), :]
    for part in range(2):
        for q in range(2):
            cols = slice(part * 1024 + q * 512, part * 1024 + q * 512 + 512)
            value = zown[7, :, cols] + crecv[7, :, cols].astype(jnp.float32)
            value = value + residual[:, cols].astype(jnp.float32)
            for way in (part, 1 - part):
                came = number(way, 1, part, q)
                arrive(rrecv.at[came], r_recv.at[came])
                value = value + rrecv[came].astype(jnp.float32)
            out_ref[:, cols] = jnp.where(alive, value, 0.0).astype(jnp.bfloat16)
    left(xg.at[0:7, 0:32], 0)
    left(xg.at[0:7, 0:32], 1)
    left(xg.at[:, 0:64], 2)
    left(rbuf, 3)
    left(keys, 4)
    left(keys.at[0:128], 5)
    left(heads.at[:, :, 0:384], 6)
    left(csend, 7)
    left(rsend, 8)


def local(hidden_in, spans, w_qkv, w_out):
    bf = jnp.bfloat16
    dma = pltpu.SemaphoreType.DMA
    vmem = pl.BlockSpec(memory_space=pltpu.VMEM)
    anyw = pl.BlockSpec(memory_space=pl.ANY)
    out = pl.pallas_call(
        block_kernel,
        out_shape=jax.ShapeDtypeStruct((64, 2048), bf),
        in_specs=[vmem, anyw, anyw, anyw],
        out_specs=vmem,
        scratch_shapes=[
            pltpu.VMEM((8, 128), jnp.int32),
            pltpu.SMEM((8, 128), jnp.int32),
            pltpu.VMEM((2 * SUBS, 128, UNIT, PIECE), bf),
            pltpu.VMEM((24576, 128), bf),
            pltpu.VMEM((384, 128), jnp.float32),
            pltpu.VMEM((12, 2048, 128), bf),
            pltpu.VMEM((512, 2048), bf),
            pltpu.VMEM((1024, 2048), bf),
            pltpu.VMEM((12, 1024, 128), bf),
            pltpu.VMEM((2, 3, GROUPS, 2, ROWS, 128), bf),
            pltpu.VMEM((2, 3, GROUPS, 3, ROWS, 128), bf),
            pltpu.VMEM((1024, 128), bf),
            pltpu.VMEM((256, UNIT, 128), bf),
            pltpu.VMEM((256, UNIT, 128), bf),
            pltpu.VMEM((2048, 128), bf),
            pltpu.VMEM((2048, 128), bf),
            pltpu.VMEM((8, 128, 2048), bf),
            pltpu.VMEM((8, 128, 1), jnp.float32),
            pltpu.VMEM((8, 128, 512), bf),
            pltpu.VMEM((8, 64, 2048), jnp.float32),
            pltpu.VMEM((8, 64, 2048), bf),
            pltpu.VMEM((8, 64, 2048), bf),
            pltpu.VMEM((28, 64, 512), bf),
            pltpu.VMEM((28, 64, 512), bf),
            dma((4,)), dma((4,)), dma((9,)),
            dma((28,)), dma((28,)), dma((1,)),
            dma((2, 3, GROUPS, 3)), dma((2, 2, GROUPS)), dma((2,)),
            dma((8,)), dma((8,)), dma((28,)),
        ],
        compiler_params=pltpu.CompilerParams(
            collective_id=1, has_side_effects=True, vmem_limit_bytes=60 * 1024 * 1024
        ),
        name="block",
    )(
        spans.T, hidden_in.reshape(8, UNIT, 2048), w_qkv.reshape(24576, 128), w_out.reshape(512, 2048)
    )
    return out[None]


def solution(mesh):
    in_specs = (P("tok", "tp"), P(), P("mod", "tp", None, "tok", None), P("mod", "tok", None, "tp"))
    out_specs = P("mod", "tok", "tp")
    return jax.shard_map(local, mesh=mesh, in_specs=in_specs, out_specs=out_specs, check_vma=False)
```

time: 112 us -> 108 us (0.964)
  Pallas kernels: 110 us -> 106 us
    pallas_call x1, Pallas kernels: 110 us -> 106 us  [local(): pl.pallas_call(block_kernel, out_shape=jax.ShapeDtypeStruct((64, 2048), b...]
where the time goes in v4:
time: 108 us
  Pallas kernels  106 us (98%)
  local copies, waits for them, and re-layouts  1.67 us (2%)
    pallas_call x1, Pallas kernels, local(): pl.pallas_call(block_kernel, out_shape=jax.ShapeDtypeStruct((64, 2048), b...  106 us

profile of v4, /device:TPU:1, one launch (start us, length us, event | category | flops | bytes accessed | tf_op | source)
XLA Modules:
  0.0 108.0 jit_solution(16128240516348515818)
XLA Ops:
  0.0 106.3 %block.1 = bf16[64,2048]{1,0:T(8,128)(2,1)} custom-call(s32[3,128]{1,0:T(4,128)} %bitcast.9, bf16[8,16,2048]{2,1,0:T(8,128)(2,1)} %bitcast.8, bf16[24576,128]{1,0:T(8,128)(2,1)} %bitcast.5, bf16[512,2048]{1,0:T(8,128)(2,1)} %bitcast.6), custom_call_target="tpu_custom_call" | custom-call | tf_op jit(solution)/shard_map/block/pallas_call | solution.py:444
  106.3 1.7 %copy.6 = bf16[1,64,2048]{2,1,0:T(8,128)(2,1)} copy(bf16[1,64,2048]{2,1,0:T(8,128)(2,1)} %bitcast.7) | data formatting | bytes 524288

commit v5 on v4

--- a/solution.py
+++ b/solution.py
@@ -180,22 +180,23 @@
     plan_copy.wait()
 
     def compact(i, carry):
-        unit = plans[1, i]
-        to = pl.ds(pl.multiple_of(i * UNIT, UNIT), UNIT)
-        for p in range(2 * SUBS):
-            xs[to, p * PIECE:(p + 1) * PIECE] = xg[p, unit]
+        for k in range(4):
+            unit = plans[1, i * 4 + k]
+            to = pl.ds(pl.multiple_of((i * 4 + k) * UNIT, UNIT), UNIT)
+            for p in range(2 * SUBS):
+                xs[to, p * PIECE:(p + 1) * PIECE] = xg[p, unit]
         return carry
 
-    lax.fori_loop(0, 64, compact, 0)
+    lax.fori_loop(0, 16, compact, 0)
 
     turn = (1, 3)
 
     def dest_of(way, step):
         return lax.rem(yp + 12 - turn[way] * (step + 1), 4)
 
-    def multiply(kind, part):
+    def multiply(kind, part, first=0, count=512):
         for way in range(2):
-            rows = slice(way * 512, way * 512 + 512)
+            rows = slice(way * 512 + first, way * 512 + first + count)
             pair = [kind * 4 + dest_of(way, 2 * part + k) for k in range(2)]
             weights = jnp.concatenate([wv[j] for j in pair], axis=1)
             value = jnp.dot(xs[rows, :], weights, preferred_element_type=jnp.float32).astype(jnp.bfloat16)
@@ -250,8 +251,9 @@
             send(reg, reg, 5, gf_recv.at[kind - 1], xdev[way])
 
     K, V, Q = 1, 2, 0
-    multiply(K, 0)
+    multiply(K, 0, 0, ROWS)
     hop(K, 0, 0)
+    multiply(K, 0, ROWS, ROWS)
     hop(K, 0, 1)
     multiply(V, 0)
     hop(V, 0, 0)

time: 108 us -> 107 us (level)
  no operation moved by 1% of the time
where the time goes in v5:
time: 107 us
  Pallas kernels  105 us (98%)
  local copies, waits for them, and re-layouts  1.67 us (2%)
    pallas_call x1, Pallas kernels, local(): pl.pallas_call(block_kernel, out_shape=jax.ShapeDtypeStruct((64, 2048), b...  105 us

profile of v5, /device:TPU:1, one launch (start us, length us, event | category | flops | bytes accessed | tf_op | source)
XLA Modules:
  0.0 107.0 jit_solution(14150901243386392142)
XLA Ops:
  0.0 105.3 %block.1 = bf16[64,2048]{1,0:T(8,128)(2,1)} custom-call(s32[3,128]{1,0:T(4,128)} %bitcast.9, bf16[8,16,2048]{2,1,0:T(8,128)(2,1)} %bitcast.8, bf16[24576,128]{1,0:T(8,128)(2,1)} %bitcast.5, bf16[512,2048]{1,0:T(8,128)(2,1)} %bitcast.6), custom_call_target="tpu_custom_call" | custom-call | tf_op jit(solution)/shard_map/block/pallas_call | solution.py:446
  105.3 1.7 %copy.6 = bf16[1,64,2048]{2,1,0:T(8,128)(2,1)} copy(bf16[1,64,2048]{2,1,0:T(8,128)(2,1)} %bitcast.7) | data formatting | bytes 524288
